TPU v7x, 32 devices: a whole 2x2x4 slice. The times are simulated.
32 devices in a mesh: dp: 32 (over z, y, x, core).
Axes of the slice: x: 2, y: 2, z: 4, core: 2. Of those that a mesh axis runs over, the one named last changes fastest.
Arguments:
- hidden_in: bfloat16 [8192, 1024], P('dp'), may hold values from -6 to 6
- segments: int32 [8192], replicated, may hold values from 0 to 47, as said below
- routes: int32 [8192, 8], P('dp'), may hold values from 0 to 31, all different within a row; in each aligned block of 256 rows (0 to 255, 256 to 511, ...) at most 80 rows name the same one
- attn_gain: float32 [1024], replicated, may hold values from 0.5 to 1.5
- w_query: bfloat16 [1024, 1024], replicated, may hold values from -0.1875 to 0.1875
- w_key: bfloat16 [1024, 512], replicated, may hold values from -0.1875 to 0.1875
- w_value: bfloat16 [1024, 512], replicated, may hold values from -0.1875 to 0.1875
- w_out: bfloat16 [1024, 1024], replicated, may hold values from -0.75 to 0.75
- moe_gain: float32 [1024], replicated, may hold values from 0.5 to 1.5
- w_router: bfloat16 [1024, 32], replicated, may hold values from -0.09375 to 0.09375
- w_gate: bfloat16 [1024, 16384], P(None, 'dp'), may hold values from -0.1875 to 0.1875
- w_up: bfloat16 [1024, 16384], P(None, 'dp'), may hold values from -0.1875 to 0.1875
- w_down: bfloat16 [16384, 1024], P('dp'), may hold values from -1 to 1
- d_out: bfloat16 [8192, 1024], P('dp'), may hold values from -6 to 6
Outputs:
- out_hidden: bfloat16 [8192, 1024], P('dp')
- grad_input: float32 [8192, 1024], P('dp')
- grad_attn_gain: float32 [1024], P('dp')
- grad_query: float32 [1024, 1024], P('dp')
- grad_key: float32 [1024, 512], P('dp')
- grad_value: float32 [1024, 512], P('dp')
- grad_out: float32 [1024, 1024], P(None, 'dp')
- grad_moe_gain: float32 [1024], P('dp')
- grad_router: float32 [1024, 32], P('dp')
- grad_gate: float32 [1024, 16384], P(None, 'dp')
- grad_up: float32 [1024, 16384], P(None, 'dp')
- grad_down: float32 [16384, 1024], P('dp')
Inputs may be any that keep to these rules, and one draw needn't show every extreme that they name: `segments`: segment numbers never fall along the tokens, and tokens of different sequences of 512 tokens have different numbers. `routes`: among the rows of one device no expert is named by more than 80 rows.
All inputs are finite; a program needn't handle non-finite values.
Results may differ from a plain program's by a relative error of at most 0.017.
Values may be sent and summed in bfloat16 or wider, within the bound.
A program may use at most 256 MiB of HBM per device.

v0:
```python
import math

import jax
import jax.numpy as jnp
from jax import lax
from jax.sharding import PartitionSpec as P

HEADS = 16
KV_HEADS = 8
HEAD_DIM = 64
TOP = 8
CAP = 80


EPSILON = 1e-06


def passed_along(value, axis, steps):
    count = lax.axis_size(axis)
    leading, last = (max(0, -steps), min(count, count - steps))
    return lax.ppermute(value, axis, [(source, source + steps) for source in range(leading, last)])


def rms_scale(values, gain):
    return values * lax.rsqrt(jnp.mean(values * values, axis=-1, keepdims=True) + EPSILON) * gain


def rope_tables(positions, head_size):
    half_size = head_size // 2
    freqs = jnp.power(10000.0, -jnp.arange(half_size, dtype=jnp.float32) / half_size)
    angles = positions.astype(jnp.float32)[:, None] * freqs[None, :]
    angles = jnp.concatenate([angles, angles], axis=1)
    return (jnp.cos(angles), jnp.sin(angles))


def rotate(values, cosine, sine):
    half_size = values.shape[-1] // 2
    turned = jnp.concatenate([-values[..., half_size:], values[..., :half_size]], axis=-1)
    return values * cosine[:, None, :] + turned * sine[:, None, :]


def unrotate(grads, cosine, sine):
    half_size = grads.shape[-1] // 2
    moved = grads * sine[:, None, :]
    return grads * cosine[:, None, :] + jnp.concatenate(
        [moved[..., half_size:], -moved[..., :half_size]], axis=-1
    )


def dot_right_t(left, right):
    return lax.dot_general(
        left, right, (((1,), (1,)), ((), ())), preferred_element_type=jnp.float32
    )


def dot_left_t(left, right):
    return lax.dot_general(
        left, right, (((0,), (0,)), ((), ())), preferred_element_type=jnp.float32
    )


def slot_table(route_rows, num_experts, capacity):
    flat_routes = route_rows.reshape(-1)
    onehot = (flat_routes[:, None] == jnp.arange(num_experts, dtype=jnp.int32)[None, :]).astype(
        jnp.int32
    )
    ranks = jnp.sum((jnp.cumsum(onehot, axis=0) - onehot) * onehot, axis=1)
    slots = flat_routes * capacity + ranks
    owners = jnp.arange(flat_routes.shape[0], dtype=jnp.int32) // route_rows.shape[1]
    token_of = jnp.zeros((num_experts * capacity,), jnp.int32).at[slots].set(owners)
    filled = jnp.zeros((num_experts * capacity,), jnp.float32).at[slots].set(1.0)
    return (slots, token_of, filled)


def block_scores(queries, key_rows, allow, score_scale):
    raw = jnp.einsum("qcgd,kcd->cgqk", queries, key_rows, preferred_element_type=jnp.float32)
    return jnp.where(allow[None, None], raw * score_scale, -1e30)


def forward_block(queries, key_rows, value_rows, allow, score_scale):
    scores = block_scores(queries, key_rows, allow, score_scale)
    row_top = jnp.max(scores, axis=-1, keepdims=True)
    weights = jnp.exp(scores - row_top)
    row_total = jnp.sum(weights, axis=-1, keepdims=True)
    probs_low = (weights / row_total).astype(jnp.bfloat16)
    attended = jnp.einsum(
        "cgqk,kcd->qcgd", probs_low, value_rows, preferred_element_type=jnp.float32
    )
    return (attended, row_top + jnp.log(row_total))


def backward_block(queries, key_rows, value_rows, allow, log_total, grad_rows, score_scale):
    scores = block_scores(queries, key_rows, allow, score_scale)
    probs = jnp.exp(scores - log_total)
    grad_probs = jnp.einsum(
        "qcgd,kcd->cgqk", grad_rows, value_rows, preferred_element_type=jnp.float32
    )
    inner = jnp.sum(probs * grad_probs, axis=-1, keepdims=True)
    grad_scores = (probs * (grad_probs - inner)).astype(jnp.bfloat16)
    grad_queries = (
        jnp.einsum("cgqk,kcd->qcgd", grad_scores, key_rows, preferred_element_type=jnp.float32)
        * score_scale
    )
    grad_keys = (
        jnp.einsum("cgqk,qcgd->kcd", grad_scores, queries, preferred_element_type=jnp.float32)
        * score_scale
    )
    grad_values = jnp.einsum(
        "cgqk,qcgd->kcd", probs.astype(jnp.bfloat16), grad_rows, preferred_element_type=jnp.float32
    )
    return (grad_queries, grad_keys, grad_values)


def local(
    hidden_in,
    segments,
    routes,
    attn_gain,
    w_query,
    w_key,
    w_value,
    w_out,
    moe_gain,
    w_router,
    w_gate,
    w_up,
    w_down,
    d_out,
):
    tok_count, model_width = hidden_in.shape
    devices = lax.axis_size("dp")
    my_index = lax.axis_index("dp")
    num_experts = w_router.shape[1]
    split_ways = devices // num_experts
    groups = HEADS // KV_HEADS
    score_scale = 1.0 / math.sqrt(HEAD_DIM)
    block_rows = min(512, tok_count)
    num_blocks = tok_count // block_rows
    places = jnp.arange(tok_count, dtype=jnp.int32)
    cosine, sine = rope_tables(my_index % 2 * tok_count + places, HEAD_DIM)
    seg_own = lax.dynamic_slice_in_dim(segments, my_index * tok_count, tok_count)
    seg_prev = lax.dynamic_slice_in_dim(
        segments, jnp.maximum(my_index - 1, 0) * tok_count, tok_count
    )
    prev_live = my_index % 2 == 1
    allow_prev = (seg_own[:, None] == seg_prev[None, :]) & prev_live
    allow_own = (seg_own[:, None] == seg_own[None, :]) & (places[None, :] <= places[:, None])
    allowed = jnp.concatenate([allow_prev, allow_own], axis=1)
    allow_blocks = allowed.reshape(num_blocks, block_rows, 2 * tok_count)
    x_float = hidden_in.astype(jnp.float32)
    h_one = rms_scale(x_float, attn_gain).astype(jnp.bfloat16)
    q_raw = jnp.dot(h_one, w_query, preferred_element_type=jnp.float32).reshape(
        tok_count, HEADS, HEAD_DIM
    )
    k_raw = jnp.dot(h_one, w_key, preferred_element_type=jnp.float32).reshape(
        tok_count, KV_HEADS, HEAD_DIM
    )
    v_low = (
        jnp.dot(h_one, w_value, preferred_element_type=jnp.float32)
        .astype(jnp.bfloat16)
        .reshape(tok_count, KV_HEADS, HEAD_DIM)
    )
    q_rot = rotate(q_raw, cosine, sine).astype(jnp.bfloat16)
    k_rot = rotate(k_raw, cosine, sine).astype(jnp.bfloat16)
    prev_keys, prev_values = passed_along((k_rot, v_low), "dp", 1)
    key_rows = jnp.concatenate([prev_keys, k_rot], axis=0)
    value_rows = jnp.concatenate([prev_values, v_low], axis=0)
    q_blocks = q_rot.reshape(num_blocks, block_rows, KV_HEADS, groups, HEAD_DIM)

    def attend(pieces):
        return forward_block(pieces[0], key_rows, value_rows, pieces[1], score_scale)

    attended, log_totals = lax.map(attend, (q_blocks, allow_blocks))
    o_low = attended.reshape(tok_count, HEADS * HEAD_DIM).astype(jnp.bfloat16)
    r_one = x_float + jnp.dot(o_low, w_out, preferred_element_type=jnp.float32)
    h_two = rms_scale(r_one, moe_gain).astype(jnp.bfloat16)
    logits = jnp.dot(h_two, w_router, preferred_element_type=jnp.float32)
    gates = jax.nn.softmax(jnp.take_along_axis(logits, routes, axis=1), axis=-1)
    slots, token_of, filled = slot_table(routes, num_experts, CAP)
    slot_rows = h_two[token_of] * filled.astype(jnp.bfloat16)[:, None]
    outgoing = jnp.broadcast_to(
        slot_rows.reshape(num_experts, 1, CAP, model_width),
        (num_experts, split_ways, CAP, model_width),
    ).reshape(devices, CAP, model_width)
    arrived = lax.all_to_all(outgoing, "dp", split_axis=0, concat_axis=0, tiled=True)
    rows = arrived.reshape(-1, model_width)
    gate_pre = jnp.dot(rows, w_gate, preferred_element_type=jnp.float32)
    up_pre = jnp.dot(rows, w_up, preferred_element_type=jnp.float32)
    hidden = (jax.nn.silu(gate_pre) * up_pre).astype(jnp.bfloat16)
    partial_out = jnp.dot(hidden, w_down, preferred_element_type=jnp.float32).astype(jnp.bfloat16)
    partial_out = partial_out.reshape(arrived.shape[0], arrived.shape[1], model_width)
    returned = lax.all_to_all(partial_out, "dp", split_axis=0, concat_axis=0, tiled=True)
    expert_slots = (
        returned.astype(jnp.float32)
        .reshape(num_experts, split_ways, CAP, model_width)
        .sum(axis=1)
        .reshape(-1, model_width)
    )
    per_route = expert_slots[slots].reshape(tok_count, TOP, model_width)
    mixed = jnp.sum(gates[:, :, None] * per_route, axis=1)
    out_hidden = (r_one + mixed).astype(jnp.bfloat16)
    cot_float = d_out.astype(jnp.float32)
    grad_gates = jnp.einsum("tjd,td->tj", per_route, cot_float)
    grad_routes = (gates[:, :, None] * cot_float[:, None, :]).astype(jnp.bfloat16)
    grad_slots = (
        jnp.zeros((num_experts * CAP, model_width), jnp.bfloat16)
        .at[slots]
        .set(grad_routes.reshape(-1, model_width))
    )
    grad_send = jnp.broadcast_to(
        grad_slots.reshape(num_experts, 1, CAP, model_width),
        (num_experts, split_ways, CAP, model_width),
    ).reshape(devices, CAP, model_width)
    arrived_grads, arrived_rows = (
        lax.all_to_all(grad_send, "dp", split_axis=0, concat_axis=0, tiled=True),
        lax.all_to_all(outgoing, "dp", split_axis=0, concat_axis=0, tiled=True),
    )
    rows = arrived_rows.reshape(-1, model_width)
    gate_pre = jnp.dot(rows, w_gate, preferred_element_type=jnp.float32)
    up_pre = jnp.dot(rows, w_up, preferred_element_type=jnp.float32)
    grad_rows = arrived_grads.reshape(-1, model_width)
    sigmoid = jax.nn.sigmoid(gate_pre)
    activated = gate_pre * sigmoid
    hidden = (jax.nn.silu(gate_pre) * up_pre).astype(jnp.bfloat16)
    grad_down = dot_left_t(hidden, grad_rows)
    grad_hidden = dot_right_t(grad_rows, w_down)
    grad_gate_pre = (grad_hidden * up_pre * (sigmoid * (1.0 + gate_pre * (1.0 - sigmoid)))).astype(
        jnp.bfloat16
    )
    grad_up_pre = (grad_hidden * activated).astype(jnp.bfloat16)
    grad_gate = dot_left_t(rows, grad_gate_pre)
    grad_up = dot_left_t(rows, grad_up_pre)
    partial_back = (dot_right_t(grad_gate_pre, w_gate) + dot_right_t(grad_up_pre, w_up)).astype(
        jnp.bfloat16
    )
    partial_back = partial_back.reshape(devices, CAP, model_width)
    returned_back = lax.all_to_all(partial_back, "dp", split_axis=0, concat_axis=0, tiled=True)
    back_slots = (
        returned_back.astype(jnp.float32)
        .reshape(num_experts, split_ways, CAP, model_width)
        .sum(axis=1)
        .reshape(-1, model_width)
    )
    grad_h_two = (
        jnp.zeros((tok_count, model_width), jnp.float32)
        .at[token_of]
        .add(back_slots * filled[:, None])
    )
    gated_sum = jnp.sum(gates * grad_gates, axis=1, keepdims=True)
    grad_sel = gates * (grad_gates - gated_sum)
    chosen = (routes[:, :, None] == jnp.arange(num_experts, dtype=jnp.int32)[None, None, :]).astype(
        jnp.float32
    )
    grad_logits = jnp.sum(grad_sel[:, :, None] * chosen, axis=1).astype(jnp.bfloat16)
    grad_router = dot_left_t(h_two, grad_logits)
    grad_h_two = grad_h_two + dot_right_t(grad_logits, w_router)
    _, norm_back_two = jax.vjp(rms_scale, r_one, moe_gain)
    grad_r_norm, grad_moe_gain = norm_back_two(grad_h_two)
    grad_r_one = cot_float + grad_r_norm
    grad_y_low = grad_r_one.astype(jnp.bfloat16)
    grad_out = dot_left_t(o_low, grad_y_low)
    grad_o_low = dot_right_t(grad_y_low, w_out).astype(jnp.bfloat16)
    grad_o_blocks = grad_o_low.reshape(num_blocks, block_rows, KV_HEADS, groups, HEAD_DIM)

    def back_step(carry, pieces):
        grad_queries, grad_keys, grad_values = backward_block(
            pieces[0], key_rows, value_rows, pieces[1], pieces[2], pieces[3], score_scale
        )
        return ((carry[0] + grad_keys, carry[1] + grad_values), grad_queries)

    zero_keys = jnp.zeros((2 * tok_count, KV_HEADS, HEAD_DIM), jnp.float32)
    (grad_key_rows, grad_value_rows), grad_q_blocks = lax.scan(
        back_step, (zero_keys, zero_keys), (q_blocks, allow_blocks, log_totals, grad_o_blocks)
    )
    back_keys, back_values = (
        passed_along(grad_key_rows[:tok_count].astype(jnp.bfloat16), "dp", -1).astype(jnp.float32),
        passed_along(grad_value_rows[:tok_count].astype(jnp.bfloat16), "dp", -1).astype(
            jnp.float32
        ),
    )
    grad_k_rot = grad_key_rows[tok_count:] + back_keys
    grad_v_rows = grad_value_rows[tok_count:] + back_values
    grad_q_rot = grad_q_blocks.reshape(tok_count, HEADS, HEAD_DIM)
    grad_q_low = (
        unrotate(grad_q_rot, cosine, sine).reshape(tok_count, HEADS * HEAD_DIM).astype(jnp.bfloat16)
    )
    grad_k_low = (
        unrotate(grad_k_rot, cosine, sine)
        .reshape(tok_count, KV_HEADS * HEAD_DIM)
        .astype(jnp.bfloat16)
    )
    grad_v_low = grad_v_rows.reshape(tok_count, KV_HEADS * HEAD_DIM).astype(jnp.bfloat16)
    grad_query = dot_left_t(h_one, grad_q_low)
    grad_key = dot_left_t(h_one, grad_k_low)
    grad_value = dot_left_t(h_one, grad_v_low)
    grad_h_one = (
        dot_right_t(grad_q_low, w_query)
        + dot_right_t(grad_k_low, w_key)
        + dot_right_t(grad_v_low, w_value)
    )
    _, norm_back_one = jax.vjp(rms_scale, x_float, attn_gain)
    grad_x_norm, grad_attn_gain = norm_back_one(grad_h_one)
    grad_input = grad_r_one + grad_x_norm
    grad_query, grad_key, grad_value, grad_out, grad_router, grad_attn_gain, grad_moe_gain = (
        lax.psum_scatter(grad_query, "dp", scatter_dimension=0, tiled=True),
        lax.psum_scatter(grad_key, "dp", scatter_dimension=0, tiled=True),
        lax.psum_scatter(grad_value, "dp", scatter_dimension=0, tiled=True),
        lax.psum_scatter(grad_out, "dp", scatter_dimension=1, tiled=True),
        lax.psum_scatter(grad_router, "dp", scatter_dimension=0, tiled=True),
        lax.psum_scatter(grad_attn_gain, "dp", scatter_dimension=0, tiled=True),
        lax.psum_scatter(grad_moe_gain, "dp", scatter_dimension=0, tiled=True),
    )
    return (
        out_hidden,
        grad_input,
        grad_attn_gain,
        grad_query,
        grad_key,
        grad_value,
        grad_out,
        grad_moe_gain,
        grad_router,
        grad_gate,
        grad_up,
        grad_down,
    )


def solution(mesh):
    return jax.shard_map(
        local,
        mesh=mesh,
        in_specs=(
            P("dp", None),
            P(),
            P("dp", None),
            P(),
            P(),
            P(),
            P(),
            P(),
            P(),
            P(),
            P(None, "dp"),
            P(None, "dp"),
            P("dp", None),
            P("dp", None),
        ),
        out_specs=(
            P("dp", None),
            P("dp", None),
            P("dp"),
            P("dp", None),
            P("dp", None),
            P("dp", None),
            P(None, "dp"),
            P("dp"),
            P("dp", None),
            P(None, "dp"),
            P(None, "dp"),
            P("dp", None),
        ),
        check_vma=False,
    )
```

profile of v0, /device:TPU:0, one launch (start us, length us, event | category | flops | bytes accessed | tf_op | source)
XLA Modules:
  0.0 1367.7 jit_solution(7187773069057861319)
XLA Ops:
  24.5 9.1 reduce-window.6
  38.4 8.2 scatter_custom_fusion
  46.7 8.3 scatter_custom_fusion.1
  72.8 8.9 gather_fusion
  84.6 120.4 %all_to_all.21 = bf16[32,80,1024]{2,1,0:T(8,128)(2,1)S(1)} all-to-all(bf16[32,80,1024]{2,1,0:T(8,128)(2,1)S(1)} %broadcast_multiply_fusion), channel_id=1, replica_groups=mesh['dp'=32] {'dp'}, dimensions={0} | all-to-all | bytes 10485760 | tf_op jit(solution)/shard_map/all_to_all | solution.py:185
  224.0 16.8 %gather_fusion.3 = f32[2048]{0:T(1024)S(1)} fusion(f32[256,32]{0,1:T(8,128)S(1)} %fusion.94, s32[2048]{0:T(1024)S(1)} %reshape.358), kind=kCustom, calls=%fused_computation.3 | custom fusion | bytes 32768 | tf_op jit(solution)/shard_map/jit(take_along_axis)/gather | solution.py:178
  241.0 98.1 %all-to-all-done.1 = bf16[32,80,1024]{2,1,0:T(8,128)(2,1)} async-done(((bf16[32,80,1024]{2,1,0:T(8,128)(2,1)}), bf16[32,80,1024]{2,1,0:T(8,128)(2,1)}, u32[]{:S(2)}, u32[]{:S(2)}) %all-to-all-start.1) | async-done | bytes 5242912 | tf_op jit(solution)/shard_map/all_to_all | solution.py:192
  339.1 14.1 %gather_fusion.2 = bf16[2048,1024]{1,0:T(8,128)(2,1)} fusion(bf16[2560,1024]{1,0:T(8,128)(2,1)} %bitcast.22, s32[2048]{0:T(1024)S(1)} %broadcast_clamp_fusion), kind=kCustom, calls=%fused_computation.2 | custom fusion | bytes 8396800 | tf_op jit(solution)/shard_map/gather | solution.py:199
  358.1 14.0 %scatter_custom_fusion.2 = bf16[2560,1024]{1,0:T(8,128)(2,1)} fusion(s32[2048]{0:T(1024)S(1)} %bitcast.215, f32[256,1024]{1,0:T(8,128)} %convert_element_type.135, f32[2048]{0:T(1024)S(1)} %mul.383, bf16[]{:T(256)} %constant.140.clone.1), kind=kCustom, calls=%fused_computation.34 | custom fusion | flops 4194304 | bytes 6299650 | tf_op jit(solution)/shard_map/scatter | solution.py:208
  372.1 119.9 %all_to_all.22 = bf16[32,80,1024]{2,1,0:T(8,128)(2,1)S(1)} all-to-all(bf16[32,80,1024]{2,1,0:T(8,128)(2,1)} %bitcast.182), channel_id=1, replica_groups=mesh['dp'=32] {'dp'}, dimensions={0} | all-to-all | bytes 10485760 | tf_op jit(solution)/shard_map/all_to_all | solution.py:215
  492.0 9.0 multiply_convert_fusion
  506.6 7.2 add_convert_fusion
  517.8 7.8 bitcast_convert_fusion
  525.6 15.8 %gather_fusion.1 = f32[2048,1024]{1,0:T(8,128)} fusion(f32[2560,1024]{1,0:T(8,128)} %bitcast_convert_fusion, s32[2048]{0:T(1024)S(1)} %broadcast_clamp_fusion), kind=kCustom, calls=%fused_computation.1 | custom fusion | bytes 16785408 | tf_op jit(solution)/shard_map/gather | solution.py:199
  542.8 6.8 fusion.5
  549.6 84.9 %all-to-all-done.3 = bf16[32,80,1024]{2,1,0:T(8,128)(2,1)} async-done(((bf16[32,80,1024]{2,1,0:T(8,128)(2,1)}), bf16[32,80,1024]{2,1,0:T(8,128)(2,1)}, u32[]{:S(2)}, u32[]{:S(2)}) %all-to-all-start.3) | async-done | bytes 5242912 | tf_op jit(solution)/shard_map/all_to_all | solution.py:237
  634.4 25.1 %scatter_custom_fusion.3 = f32[256,1024]{1,0:T(8,128)} fusion(f32[256,1024]{1,0:T(8,128)} %fusion.102, s32[2560]{0:T(1024)} %copy-done.44, bf16[2560,1024]{1,0:T(8,128)(2,1)} %bitcast.51, f32[2560]{0:T(1024)S(1)} %copy-done.40), kind=kCustom, calls=%fused_computation.9 | custom fusion | flops 7864320 | bytes 6301696 | tf_op jit(solution)/shard_map/scatter-add | solution.py:247
  715.2 7.6 fusion.100
  734.4 45.7 %all-reduce.2 = (f32[1024]{0:T(1024)S(1)}, f32[1024]{0:T(1024)S(1)}) all-reduce(f32[1024]{0:T(1024)S(1)} %get-tuple-element.55, f32[1024]{0:T(1024)S(1)} %get-tuple-element.53), channel_id=2, replica_groups=mesh['dp'=32] {'dp'}, use_global_device_ids=true, to_apply=%region_20.21.clone | all-reduce | flops 2048 | bytes 16384
  784.1 26.2 %reduce-scatter.14.cloned.1.call-done = f32[32,32]{1,0:T(8,128)} async-done(((f32[1024,32]{1,0:T(8,128)}), f32[32,32]{1,0:T(8,128)}) %reduce-scatter.14.cloned.1.call-update) | async-done | bytes 4112 | tf_op jit(solution)/shard_map/reduce_scatter | solution.py:309
  810.3 135.7 %reduce-scatter.10.cloned.1.call-done = f32[32,512]{1,0:T(8,128)} async-done(((f32[1024,512]{1,0:T(8,128)}), f32[32,512]{1,0:T(8,128)}) %reduce-scatter.10.cloned.1.call-update) | async-done | bytes 65552 | tf_op jit(solution)/shard_map/reduce_scatter | solution.py:307
  945.9 135.5 %reduce-scatter.8.cloned.1.call-done = f32[32,512]{1,0:T(8,128)} async-done(((f32[1024,512]{1,0:T(8,128)}), f32[32,512]{1,0:T(8,128)}) %reduce-scatter.8.cloned.1.call-update) | async-done | bytes 65552 | tf_op jit(solution)/shard_map/reduce_scatter | solution.py:306
  1081.4 139.7 %reduce-scatter.12.cloned.1.call-done = f32[1024,32]{0,1:T(8,128)} async-done(((f32[1024,1024]{0,1:T(8,128)}), f32[1024,32]{0,1:T(8,128)}) %reduce-scatter.12.cloned.1.call-update) | async-done | bytes 131088 | tf_op jit(solution)/shard_map/reduce_scatter | solution.py:308
  1221.2 139.6 %reduce-scatter.6.cloned.1.call-done = f32[32,1024]{1,0:T(8,128)} async-done(((f32[1024,1024]{1,0:T(8,128)}), f32[32,1024]{1,0:T(8,128)}) %reduce-scatter.6.cloned.1.call-update) | async-done | bytes 131088 | tf_op jit(solution)/shard_map/reduce_scatter | solution.py:305
  (253 shorter events, 148.0 us)
Async XLA Ops:
  7.2 63.6 %copy-start = (bf16[1024,1024]{1,0:T(8,128)(2,1)S(1)}, bf16[1024,1024]{1,0:T(8,128)(2,1)}, u32[]{:S(2)}) copy-start(bf16[1024,1024]{1,0:T(8,128)(2,1)} %param.21) | copy-start | bytes 6291460
  9.2 47.1 %copy-start.41 = (f32[256]{0:T(256)}, f32[256]{0:T(256)S(1)}, u32[]{:S(2)}) copy-start(f32[256]{0:T(256)S(1)} %fusion.71) | copy-start | bytes 3076
  9.2 47.1 %copy-start.4 = (bf16[256,1024]{1,0:T(8,128)(2,1)S(1)}, bf16[256,1024]{1,0:T(8,128)(2,1)}, u32[]{:S(2)}) copy-start(bf16[256,1024]{1,0:T(8,128)(2,1)} %param.14) | copy-start | bytes 1572868
  9.2 47.1 %copy-start.37 = (f32[1024]{0:T(1024)S(1)}, f32[1024]{0:T(1024)}, u32[]{:S(2)}) copy-start(f32[1024]{0:T(1024)} %param.17) | copy-start | bytes 12292
  12.0 55.8 %collective-permute-start = (bf16[256,8,64]{0,2,1:T(8,128)(2,1)}, bf16[256,8,64]{0,2,1:T(8,128)(2,1)}, u32[]{:S(2)}, u32[]{:S(2)}) collective-permute-start(bf16[256,8,64]{0,2,1:T(8,128)(2,1)} %bitcast), channel_id=1, source_target_pairs={{0,1},{1,2},{2,3},{3,4},{4,5},{5,6},{6,7},{7,8},{8,9},{9,10},{10,1... | collective-permute-start | bytes 786440 | tf_op jit(solution)/shard_map/ppermute | solution.py:21
  15.2 46.5 %copy-start.29 = (f32[256,64]{0,1:T(8,128)}, f32[256,64]{0,1:T(8,128)S(1)}, u32[]{:S(2)}) copy-start(f32[256,64]{0,1:T(8,128)S(1)} %get-tuple-element.84) | copy-start | bytes 196612
  15.3 46.5 %copy-start.31 = (f32[256,64]{0,1:T(8,128)}, f32[256,64]{0,1:T(8,128)S(1)}, u32[]{:S(2)}) copy-start(f32[256,64]{0,1:T(8,128)S(1)} %get-tuple-element.83) | copy-start | bytes 196612
  17.5 45.9 %collective-permute-start.1 = (bf16[256,8,64]{0,2,1:T(8,128)(2,1)S(1)}, bf16[256,8,64]{0,2,1:T(8,128)(2,1)}, u32[]{:S(2)}, u32[]{:S(2)}) collective-permute-start(bf16[256,8,64]{0,2,1:T(8,128)(2,1)S(1)} %fusion.42), channel_id=1, source_target_pairs={{0,1},{1,2},{2,3},{3,4},{4,5},{5,6},{6,7},{7,8},{8,9},{9,10},{10,1... | collective-permute-start | bytes 786440 | tf_op jit(solution)/shard_map/ppermute | solution.py:21
  84.6 120.4 %copy-start.58 = (bf16[1024,512]{1,0:T(8,128)(2,1)S(1)}, bf16[1024,512]{1,0:T(8,128)(2,1)}, u32[]{:S(2)}) copy-start(bf16[1024,512]{1,0:T(8,128)(2,1)} %param.24) | copy-start | bytes 3145732
  218.0 121.1 %all-to-all-start.1 = ((bf16[32,80,1024]{2,1,0:T(8,128)(2,1)}), bf16[32,80,1024]{2,1,0:T(8,128)(2,1)}, u32[]{:S(2)}, u32[]{:S(2)}) async-start(bf16[32,80,1024]{2,1,0:T(8,128)(2,1)} %bitcast.189), calls=%async_computation.1 | async-start | bytes 10485760 | tf_op jit(solution)/shard_map/all_to_all | solution.py:192
  372.1 119.9 %copy-start.57 = (bf16[512,1024]{1,0:T(8,128)(2,1)S(1)}, bf16[512,1024]{1,0:T(8,128)(2,1)}, u32[]{:S(2)}) copy-start(bf16[512,1024]{1,0:T(8,128)(2,1)} %param.26) | copy-start | bytes 3145732
  513.8 120.6 %all-to-all-start.3 = ((bf16[32,80,1024]{2,1,0:T(8,128)(2,1)}), bf16[32,80,1024]{2,1,0:T(8,128)(2,1)}, u32[]{:S(2)}, u32[]{:S(2)}) async-start(bf16[32,80,1024]{2,1,0:T(8,128)(2,1)} %bitcast.188), calls=%async_computation.3 | async-start | bytes 10485760 | tf_op jit(solution)/shard_map/all_to_all | solution.py:237
  517.7 292.6 %reduce-scatter.14.cloned.1.call-start = ((), (), s32[]{:S(2)}) async-start(), calls=%async_computation.13 | async-start | bytes 540672 | tf_op jit(solution)/shard_map/reduce_scatter | solution.py:309
  541.5 93.0 %copy-start.40 = (f32[2560]{0:T(1024)S(1)}, f32[2560]{0:T(1024)}, u32[]{:S(2)}) copy-start(f32[2560]{0:T(1024)} %copy-done.39) | copy-start | bytes 30724
  549.6 110.0 %copy-start.46 = (f32[1024]{0:T(1024)S(1)}, f32[1024]{0:T(1024)}, u32[]{:S(2)}) copy-start(f32[1024]{0:T(1024)} %param.22) | copy-start | bytes 12292
  549.6 110.0 %copy-start.51 = (f32[256]{0:T(256)S(1)}, f32[256]{0:T(256)}, u32[]{:S(2)}) copy-start(f32[256]{0:T(256)} %copy-done.50) | copy-start | bytes 3076
  549.6 111.8 %copy-start.55 = (f32[256]{0:T(256)S(1)}, f32[256]{0:T(256)}, u32[]{:S(2)}) copy-start(f32[256]{0:T(256)} %copy-done.54) | copy-start | bytes 3076
  673.2 3.6 collective-permute-start.3
  675.7 270.3 %reduce-scatter.10.cloned.1.call-start = ((), (), s32[]{:S(2)}) async-start(), calls=%async_computation.11 | async-start | bytes 2162688 | tf_op jit(solution)/shard_map/reduce_scatter | solution.py:307
  679.9 401.5 %reduce-scatter.8.cloned.1.call-start = ((), (), s32[]{:S(2)}) async-start(), calls=%async_computation.10 | async-start | bytes 2162688 | tf_op jit(solution)/shard_map/reduce_scatter | solution.py:306
  694.0 7.0 collective-permute-start.2
  703.8 517.3 %reduce-scatter.12.cloned.1.call-start = ((), (), s32[]{:S(2)}) async-start(), calls=%async_computation.12 | async-start | bytes 4325376 | tf_op jit(solution)/shard_map/reduce_scatter | solution.py:308
  707.9 652.9 %reduce-scatter.6.cloned.1.call-start = ((), (), s32[]{:S(2)}) async-start(), calls=%async_computation.9 | async-start | bytes 4325376 | tf_op jit(solution)/shard_map/reduce_scatter | solution.py:305
  731.4 49.9 %copy-start.53 = (f32[256]{0:T(256)S(1)}, f32[256]{0:T(256)}, u32[]{:S(2)}) copy-start(f32[256]{0:T(256)} %copy-done.52) | copy-start | bytes 3076
  (53 other events, 333.7 us)
Sparse Core Ops, SparseCore 0:
  675.8 134.4 reduce-scatter.13
  813.2 132.6 reduce-scatter.9
  948.8 132.6 reduce-scatter.7
  1084.2 136.8 reduce-scatter.11
  1224.0 136.7 reduce-scatter.5
where the time goes:
time: 1370 us
  waiting for transfers between devices  766 us (56%)
  blocking collectives  286 us (21%)
  matrix products  100 us (7%)
  other arithmetic  91.9 us (7%)
  local copies, waits for them, and re-layouts  89.3 us (7%)
  starting transfers between devices  19 us (1%)
  between operations  15.2 us (1%)
    reduce_scatter x1, waiting for transfers between devices, local(): lax.psum_scatter(grad_out, 'dp', scatter_dimension=1, tiled=True)  140 us
    reduce_scatter x1, waiting for transfers between devices, local(): lax.psum_scatter(grad_query, 'dp', scatter_dimension=0, tiled=True)  140 us
    reduce_scatter x1, waiting for transfers between devices, local(): lax.psum_scatter(grad_value, 'dp', scatter_dimension=0, tiled=True)  136 us
    reduce_scatter x1, waiting for transfers between devices, local(): lax.psum_scatter(grad_key, 'dp', scatter_dimension=0, tiled=True)  135 us
    all_to_all x1, blocking collectives, local(): lax.all_to_all(outgoing, 'dp', split_axis=0, concat_axis=0, tiled=True)  120 us
    all_to_all x1, blocking collectives, local(): lax.all_to_all(grad_send, 'dp', split_axis=0, concat_axis=0, tiled=True)  120 us
    all_to_all x1, waiting for transfers between devices, local(): lax.all_to_all(partial_out, 'dp', split_axis=0, concat_axis=0, tiled=True)  98.1 us
    all_to_all x1, waiting for transfers between devices, local(): lax.all_to_all(partial_back, 'dp', split_axis=0, concat_axis=0, tiled=True)  84.9 us
  transfers between devices with their start and end apart: 11, of which 9 were waited for; matrix products, arithmetic and copies ran while one was open for 11% of the time, Pallas kernels for 0%

commit v1 on v0

v1 whole, which is shorter than its diff:
```python
import math

import jax
import jax.numpy as jnp
from jax import lax
from jax.sharding import PartitionSpec as P

HEADS = 16
KV_HEADS = 8
HEAD_DIM = 64
TOP = 8
CAP = 80


EPSILON = 1e-06


def passed_along(value, axis, steps):
    count = lax.axis_size(axis)
    leading, last = (max(0, -steps), min(count, count - steps))
    return lax.ppermute(value, axis, [(source, source + steps) for source in range(leading, last)])


def rms_scale(values, gain):
    return values * lax.rsqrt(jnp.mean(values * values, axis=-1, keepdims=True) + EPSILON) * gain


def rope_tables(positions, head_size):
    half_size = head_size // 2
    freqs = jnp.power(10000.0, -jnp.arange(half_size, dtype=jnp.float32) / half_size)
    angles = positions.astype(jnp.float32)[:, None] * freqs[None, :]
    angles = jnp.concatenate([angles, angles], axis=1)
    return (jnp.cos(angles), jnp.sin(angles))


def rotate(values, cosine, sine):
    half_size = values.shape[-1] // 2
    turned = jnp.concatenate([-values[..., half_size:], values[..., :half_size]], axis=-1)
    return values * cosine[:, None, :] + turned * sine[:, None, :]


def unrotate(grads, cosine, sine):
    half_size = grads.shape[-1] // 2
    moved = grads * sine[:, None, :]
    return grads * cosine[:, None, :] + jnp.concatenate(
        [moved[..., half_size:], -moved[..., :half_size]], axis=-1
    )


def dot_right_t(left, right):
    return lax.dot_general(
        left, right, (((1,), (1,)), ((), ())), preferred_element_type=jnp.float32
    )


def dot_left_t(left, right):
    return lax.dot_general(
        left, right, (((0,), (0,)), ((), ())), preferred_element_type=jnp.float32
    )


def split_two(values):
    high = values.astype(jnp.bfloat16)
    rest = (values - high.astype(jnp.float32)).astype(jnp.bfloat16)
    return high, rest


def member_mask(route_rows, num_experts):
    ids = jnp.arange(num_experts, dtype=jnp.int32)
    return jnp.any(route_rows[:, :, None] == ids[None, None, :], axis=1)


def placement(mask, first, amount):
    tok_count = mask.shape[0]
    part = lax.dynamic_slice_in_dim(mask.astype(jnp.bfloat16), first, amount, axis=1)
    places = jnp.arange(tok_count, dtype=jnp.int32)
    earlier = (places[:, None] < places[None, :]).astype(jnp.bfloat16)
    ranks = dot_left_t(part, earlier)
    ranks = jnp.where(part.T > 0, ranks, -1.0)
    want = jnp.arange(CAP, dtype=jnp.int32).astype(jnp.float32)
    chosen = (ranks[:, None, :] == want[None, :, None]).astype(jnp.bfloat16)
    return chosen.reshape(amount * CAP, tok_count)


def spread(chosen, values, amount, split_ways, groups):
    width = values.shape[1]
    picked = jnp.dot(chosen, values, preferred_element_type=jnp.float32).astype(jnp.bfloat16)
    sent = jnp.broadcast_to(
        picked.reshape(amount, 1, CAP, width), (amount, split_ways, CAP, width)
    ).reshape(amount * split_ways, CAP, width)
    return lax.all_to_all(
        sent, "dp", split_axis=0, concat_axis=0, tiled=True, axis_index_groups=groups
    ).reshape(-1, width)


def bring_back(chosen, rows, amount, split_ways, groups):
    width = rows.shape[1]
    back = lax.all_to_all(
        rows.reshape(amount * split_ways, CAP, width),
        "dp",
        split_axis=0,
        concat_axis=0,
        tiled=True,
        axis_index_groups=groups,
    ).reshape(-1, width)
    if split_ways > 1:
        tok_count = chosen.shape[1]
        chosen = jnp.broadcast_to(
            chosen.reshape(amount, 1, CAP, tok_count), (amount, split_ways, CAP, tok_count)
        ).reshape(-1, tok_count)
    return back, chosen


def expert_block(rows, gate, cot_rows, w_gate, w_up, w_down):
    gate_pre = jnp.dot(rows, w_gate, preferred_element_type=jnp.float32)
    up_pre = jnp.dot(rows, w_up, preferred_element_type=jnp.float32)
    sigmoid = jax.nn.sigmoid(gate_pre)
    activated = gate_pre * sigmoid
    hidden = (activated * up_pre).astype(jnp.bfloat16)
    cot_float = cot_rows.astype(jnp.float32)
    grad_rows = (gate * cot_float).astype(jnp.bfloat16)
    grad_hidden = dot_right_t(grad_rows, w_down)
    grad_gate_pre = (grad_hidden * up_pre * (sigmoid * (1.0 + gate_pre * (1.0 - sigmoid)))).astype(
        jnp.bfloat16
    )
    grad_up_pre = (grad_hidden * activated).astype(jnp.bfloat16)
    back = (dot_right_t(grad_gate_pre, w_gate) + dot_right_t(grad_up_pre, w_up)).astype(
        jnp.bfloat16
    )
    expert_out = jnp.dot(hidden, w_down, preferred_element_type=jnp.float32)
    grad_gates = jnp.sum(expert_out * cot_float, axis=1, keepdims=True)
    gated_out = (gate * expert_out).astype(jnp.bfloat16)
    return (hidden, grad_rows, grad_gate_pre, grad_up_pre, back, grad_gates, gated_out)


def reduced(parts, extras, devices):
    sizes = (2, 4, devices // 8)
    rows = parts.shape[0] // devices
    width = parts.shape[1]
    extra_width = extras.shape[1]
    filler = jnp.zeros((parts.shape[0], 128 - 2 * extra_width), jnp.bfloat16)
    grid = (sizes[2], sizes[1], sizes[0], rows, -1)
    main, extra = parts.reshape(grid), extras.reshape(grid)
    filler = filler.reshape(grid)
    stage_groups = (
        [[2 * i, 2 * i + 1] for i in range(devices // 2)],
        [[8 * z + 2 * i + c for i in range(4)] for z in range(devices // 8) for c in range(2)],
        [[8 * z + i for z in range(devices // 8)] for i in range(8)],
    )
    for groups, size in zip(stage_groups, sizes):
        high, rest = split_two(extra)
        packed = jnp.concatenate([main.astype(jnp.bfloat16), high, rest, filler], axis=-1)
        axis = packed.ndim - 3
        packed = jnp.moveaxis(packed, axis, 0)
        got = lax.all_to_all(
            packed, "dp", split_axis=0, concat_axis=0, tiled=True, axis_index_groups=groups
        )
        total = jnp.sum(got.astype(jnp.float32), axis=0)
        main = total[..., :width]
        extra = (
            total[..., width : width + extra_width]
            + total[..., width + extra_width : width + 2 * extra_width]
        )
        filler = filler.reshape((-1,) + filler.shape[-2:])[: math.prod(total.shape[:-2])]
        filler = filler.reshape(total.shape[:-1] + (filler.shape[-1],))
    return main, extra


def block_scores(queries, key_rows, allow, score_scale):
    raw = jnp.einsum("qcgd,kcd->cgqk", queries, key_rows, preferred_element_type=jnp.float32)
    return jnp.where(allow[None, None], raw * score_scale, -1e30)


def forward_block(queries, key_rows, value_rows, allow, score_scale):
    scores = block_scores(queries, key_rows, allow, score_scale)
    row_top = jnp.max(scores, axis=-1, keepdims=True)
    weights = jnp.exp(scores - row_top)
    row_total = jnp.sum(weights, axis=-1, keepdims=True)
    probs_low = (weights / row_total).astype(jnp.bfloat16)
    attended = jnp.einsum(
        "cgqk,kcd->qcgd", probs_low, value_rows, preferred_element_type=jnp.float32
    )
    return (attended, row_top + jnp.log(row_total))


def backward_block(queries, key_rows, value_rows, allow, log_total, grad_rows, score_scale):
    scores = block_scores(queries, key_rows, allow, score_scale)
    probs = jnp.exp(scores - log_total)
    grad_probs = jnp.einsum(
        "qcgd,kcd->cgqk", grad_rows, value_rows, preferred_element_type=jnp.float32
    )
    inner = jnp.sum(probs * grad_probs, axis=-1, keepdims=True)
    grad_scores = (probs * (grad_probs - inner)).astype(jnp.bfloat16)
    grad_queries = (
        jnp.einsum("cgqk,kcd->qcgd", grad_scores, key_rows, preferred_element_type=jnp.float32)
        * score_scale
    )
    grad_keys = (
        jnp.einsum("cgqk,qcgd->kcd", grad_scores, queries, preferred_element_type=jnp.float32)
        * score_scale
    )
    grad_values = jnp.einsum(
        "cgqk,qcgd->kcd", probs.astype(jnp.bfloat16), grad_rows, preferred_element_type=jnp.float32
    )
    return (grad_queries, grad_keys, grad_values)


def local(
    hidden_in,
    segments,
    routes,
    attn_gain,
    w_query,
    w_key,
    w_value,
    w_out,
    moe_gain,
    w_router,
    w_gate,
    w_up,
    w_down,
    d_out,
):
    tok_count, model_width = hidden_in.shape
    devices = lax.axis_size("dp")
    my_index = lax.axis_index("dp")
    num_experts = w_router.shape[1]
    split_ways = devices // num_experts
    groups = HEADS // KV_HEADS
    score_scale = 1.0 / math.sqrt(HEAD_DIM)
    places = jnp.arange(tok_count, dtype=jnp.int32)
    cosine, sine = rope_tables(my_index % 2 * tok_count + places, HEAD_DIM)
    seg_own = lax.dynamic_slice_in_dim(segments, my_index * tok_count, tok_count)
    seg_prev = lax.dynamic_slice_in_dim(
        segments, jnp.maximum(my_index - 1, 0) * tok_count, tok_count
    )
    prev_live = my_index % 2 == 1
    allow_prev = (seg_own[:, None] == seg_prev[None, :]) & prev_live
    allow_own = (seg_own[:, None] == seg_own[None, :]) & (places[None, :] <= places[:, None])
    allowed = jnp.concatenate([allow_prev, allow_own], axis=1)
    half_devices = devices // 2
    half_experts = num_experts // 2
    half = my_index // half_devices
    half_groups = [list(range(half_devices)), list(range(half_devices, devices))]
    across = [(i, (i + half_devices) % devices) for i in range(devices)]
    my_expert = my_index // split_ways
    far_routes, far_cot = lax.ppermute((routes, d_out), "dp", across)
    near_mask = member_mask(routes, num_experts)
    near_place = placement(near_mask, half * half_experts, half_experts)
    far_place = placement(
        member_mask(far_routes, num_experts), half * half_experts, half_experts
    )
    near_cot_rows = spread(near_place, d_out, half_experts, split_ways, half_groups)
    far_cot_rows = spread(far_place, far_cot, half_experts, split_ways, half_groups)
    x_float = hidden_in.astype(jnp.float32)
    h_one = rms_scale(x_float, attn_gain).astype(jnp.bfloat16)
    q_raw = jnp.dot(h_one, w_query, preferred_element_type=jnp.float32).reshape(
        tok_count, HEADS, HEAD_DIM
    )
    k_raw = jnp.dot(h_one, w_key, preferred_element_type=jnp.float32).reshape(
        tok_count, KV_HEADS, HEAD_DIM
    )
    v_low = (
        jnp.dot(h_one, w_value, preferred_element_type=jnp.float32)
        .astype(jnp.bfloat16)
        .reshape(tok_count, KV_HEADS, HEAD_DIM)
    )
    q_rot = rotate(q_raw, cosine, sine).astype(jnp.bfloat16)
    k_rot = rotate(k_raw, cosine, sine).astype(jnp.bfloat16)
    prev_keys, prev_values = passed_along((k_rot, v_low), "dp", 1)
    key_rows = jnp.concatenate([prev_keys, k_rot], axis=0)
    value_rows = jnp.concatenate([prev_values, v_low], axis=0)
    q_blocks = q_rot.reshape(tok_count, KV_HEADS, groups, HEAD_DIM)

    attended, log_total = forward_block(q_blocks, key_rows, value_rows, allowed, score_scale)
    o_low = attended.reshape(tok_count, HEADS * HEAD_DIM).astype(jnp.bfloat16)
    r_one = x_float + jnp.dot(o_low, w_out, preferred_element_type=jnp.float32)
    h_two = rms_scale(r_one, moe_gain).astype(jnp.bfloat16)
    logits = jnp.dot(h_two, w_router, preferred_element_type=jnp.float32)
    gates = jax.nn.softmax(jnp.where(near_mask, logits, -jnp.inf), axis=-1)
    gate_high, gate_rest = split_two(gates)
    pad = jnp.zeros((tok_count, 128 - 2 * num_experts), jnp.bfloat16)
    near_tokens = jnp.concatenate([h_two, gate_high, gate_rest, pad], axis=1)
    far_tokens = lax.ppermute(near_tokens, "dp", across)
    near_rows = spread(near_place, near_tokens, half_experts, split_ways, half_groups)
    far_rows = spread(far_place, far_tokens, half_experts, split_ways, half_groups)
    lane = jnp.arange(128, dtype=jnp.int32)
    lane_high = (lane == my_expert)[None, :]
    lane_rest = (lane == my_expert + num_experts)[None, :]

    def work(rows, cot_rows):
        tail = rows[:, model_width:].astype(jnp.float32)
        gate = jnp.sum(jnp.where(lane_high | lane_rest, tail, 0.0), axis=1, keepdims=True)
        rows = rows[:, :model_width]
        results = expert_block(rows, gate, cot_rows, w_gate, w_up, w_down)
        high, rest = split_two(results[5])
        extra = jnp.where(lane_high, high, jnp.where(lane_rest, rest, jnp.bfloat16(0)))
        return (rows,) + results[:4] + (jnp.concatenate([results[4], extra], axis=1), results[6])

    near = work(near_rows, near_cot_rows)
    far = work(far_rows, far_cot_rows)

    def combine(back, chosen):
        return dot_left_t(chosen, back)

    far_back, far_wide = bring_back(far_place, far[5], half_experts, split_ways, half_groups)
    near_back, near_wide = bring_back(near_place, near[5], half_experts, split_ways, half_groups)
    far_sum = lax.ppermute(combine(far_back, far_wide).astype(jnp.bfloat16), "dp", across)
    grad_tokens = combine(near_back, near_wide) + far_sum.astype(jnp.float32)
    near_out, far_out, _ = lax.optimization_barrier((near[6], far[6], near_back))
    far_ret, _ = bring_back(far_place, far_out, half_experts, split_ways, half_groups)
    near_ret, _ = bring_back(near_place, near_out, half_experts, split_ways, half_groups)
    far_mix = lax.ppermute(combine(far_ret, far_wide).astype(jnp.bfloat16), "dp", across)
    mixed = combine(near_ret, near_wide) + far_mix.astype(jnp.float32)
    out_hidden = (r_one + mixed).astype(jnp.bfloat16)
    grad_down = dot_left_t(near[1], near[2]) + dot_left_t(far[1], far[2])
    grad_gate = dot_left_t(near[0], near[3]) + dot_left_t(far[0], far[3])
    grad_up = dot_left_t(near[0], near[4]) + dot_left_t(far[0], far[4])
    cot_float = d_out.astype(jnp.float32)
    grad_h_two = grad_tokens[:, :model_width]
    grad_gates = (
        grad_tokens[:, model_width : model_width + num_experts]
        + grad_tokens[:, model_width + num_experts : model_width + 2 * num_experts]
    )
    gated_sum = jnp.sum(gates * grad_gates, axis=1, keepdims=True)
    grad_logits = (gates * (grad_gates - gated_sum)).astype(jnp.bfloat16)
    grad_router = dot_left_t(h_two, grad_logits)
    grad_h_two = grad_h_two + dot_right_t(grad_logits, w_router)
    _, norm_back_two = jax.vjp(rms_scale, r_one, moe_gain)
    grad_r_norm, grad_moe_gain = norm_back_two(grad_h_two)
    grad_r_one = cot_float + grad_r_norm
    grad_y_low = grad_r_one.astype(jnp.bfloat16)
    grad_out_t = dot_left_t(grad_y_low, o_low)
    out_part, out_extra = reduced(
        grad_out_t, jnp.concatenate([grad_router, grad_moe_gain[:, None]], axis=1), devices
    )
    grad_o_low = dot_right_t(grad_y_low, w_out).astype(jnp.bfloat16)
    grad_o_blocks = grad_o_low.reshape(tok_count, KV_HEADS, groups, HEAD_DIM)
    grad_q_blocks, grad_key_rows, grad_value_rows = backward_block(
        q_blocks, key_rows, value_rows, allowed, log_total, grad_o_blocks, score_scale
    )
    back_keys, back_values = (
        passed_along(grad_key_rows[:tok_count].astype(jnp.bfloat16), "dp", -1).astype(jnp.float32),
        passed_along(grad_value_rows[:tok_count].astype(jnp.bfloat16), "dp", -1).astype(
            jnp.float32
        ),
    )
    grad_k_rot = grad_key_rows[tok_count:] + back_keys
    grad_v_rows = grad_value_rows[tok_count:] + back_values
    grad_q_rot = grad_q_blocks.reshape(tok_count, HEADS, HEAD_DIM)
    grad_q_low = (
        unrotate(grad_q_rot, cosine, sine).reshape(tok_count, HEADS * HEAD_DIM).astype(jnp.bfloat16)
    )
    grad_k_low = (
        unrotate(grad_k_rot, cosine, sine)
        .reshape(tok_count, KV_HEADS * HEAD_DIM)
        .astype(jnp.bfloat16)
    )
    grad_v_low = grad_v_rows.reshape(tok_count, KV_HEADS * HEAD_DIM).astype(jnp.bfloat16)
    grad_query = dot_left_t(h_one, grad_q_low)
    grad_key = dot_left_t(h_one, grad_k_low)
    grad_value = dot_left_t(h_one, grad_v_low)
    grad_h_one = (
        dot_right_t(grad_q_low, w_query)
        + dot_right_t(grad_k_low, w_key)
        + dot_right_t(grad_v_low, w_value)
    )
    _, norm_back_one = jax.vjp(rms_scale, x_float, attn_gain)
    grad_x_norm, grad_attn_gain = norm_back_one(grad_h_one)
    grad_input = grad_r_one + grad_x_norm
    shared = jnp.concatenate([grad_query, grad_key, grad_value], axis=1)
    shared_part, shared_extra = reduced(shared, grad_attn_gain[:, None], devices)
    query_width, key_width = grad_query.shape[1], grad_key.shape[1]
    grad_query = shared_part[:, :query_width]
    grad_key = shared_part[:, query_width : query_width + key_width]
    grad_value = shared_part[:, query_width + key_width :]
    grad_attn_gain = shared_extra[:, 0]
    grad_out = out_part.T
    grad_router = out_extra[:, :num_experts]
    grad_moe_gain = out_extra[:, num_experts]
    return (
        out_hidden,
        grad_input,
        grad_attn_gain,
        grad_query,
        grad_key,
        grad_value,
        grad_out,
        grad_moe_gain,
        grad_router,
        grad_gate,
        grad_up,
        grad_down,
    )


def solution(mesh):
    return jax.shard_map(
        local,
        mesh=mesh,
        in_specs=(
            P("dp", None),
            P(),
            P("dp", None),
            P(),
            P(),
            P(),
            P(),
            P(),
            P(),
            P(),
            P(None, "dp"),
            P(None, "dp"),
            P("dp", None),
            P("dp", None),
        ),
        out_specs=(
            P("dp", None),
            P("dp", None),
            P("dp"),
            P("dp", None),
            P("dp", None),
            P("dp", None),
            P(None, "dp"),
            P("dp"),
            P("dp", None),
            P(None, "dp"),
            P(None, "dp"),
            P("dp", None),
        ),
        check_vma=False,
    )
```

time: 1370 us -> 636 us (0.46)
  waiting for transfers between devices: 766 us -> 214 us
  blocking collectives: 286 us -> 36.6 us
  starting transfers between devices: 19 us -> 95.1 us
  other arithmetic: 91.9 us -> 46.8 us
  matrix products: 100 us -> 131 us
    reduce_scatter x5 -> x0, waiting for transfers between devices: 577 us -> none  [the longest x1 140 us: local(): lax.psum_scatter(grad_out, 'dp', scatter_dimension=1, tiled=True)]
    all_to_all x2, blocking collectives: 240 us -> 36.6 us  [reduced(): lax.all_to_all(packed, 'dp', split_axis=0, concat_axis=0, tiled=True, axi...]
    ppermute x0 -> x5, waiting for transfers between devices: none -> 89.2 us  [the longest x1 54.4 us: local(): far_tokens = lax.ppermute(near_tokens, 'dp', across)]
    all_to_all x2 -> x12, starting transfers between devices: 8.23 us -> 67.8 us  [the longest x4 27.1 us: bring_back(): lax.all_to_all(rows.reshape(amount * split_ways, CAP, width), 'dp', split...]
    all_to_all x2 -> x12, waiting for transfers between devices: 183 us -> 125 us  [the longest x4 76.6 us: bring_back(): lax.all_to_all(rows.reshape(amount * split_ways, CAP, width), 'dp', split...]
    gather x8 -> x0, local copies, waits for them, and re-layouts: 56.1 us -> none  [the longest x2 30 us: local(): per_route = expert_slots[slots].reshape(tok_count, TOP, model_width)]
    unnamed x1 -> x0, blocking collectives: 45.7 us -> none
    concatenate x0 -> x11, local copies, waits for them, and re-layouts: none -> 43.4 us  [the longest x6 22.4 us: reduced(): jnp.concatenate([main.astype(jnp.bfloat16), high, rest, filler], axis=-1)]
  transfers between devices with their start and end apart: 11 -> 21, of which waited for: 9 -> 11; matrix products, arithmetic and copies ran while one was open for 11% -> 32% of each run, Pallas kernels for 0% -> 0%
where the time goes in v1:
time: 636 us; the launch traced here: 628 us
  waiting for transfers between devices  214 us (34%)
  matrix products  131 us (21%)
  local copies, waits for them, and re-layouts  102 us (16%)
  starting transfers between devices  95.1 us (15%)
  other arithmetic  46.8 us (7%)
  blocking collectives  36.6 us (6%)
    all_to_all x4, waiting for transfers between devices, bring_back(): lax.all_to_all(rows.reshape(amount * split_ways, CAP, width), 'dp', split...  76.6 us
    ppermute x1, waiting for transfers between devices, local(): far_tokens = lax.ppermute(near_tokens, 'dp', across)  54.4 us
    dot_general x17, matrix products, dot_left_t(): lax.dot_general(left, right, (((0,), (0,)), ((), ())), preferred_element_...  46.3 us
    all_to_all x2, blocking collectives, reduced(): lax.all_to_all(packed, 'dp', split_axis=0, concat_axis=0, tiled=True, axi...  36.6 us
    ppermute x2, waiting for transfers between devices, local(): far_routes, far_cot = lax.ppermute((routes, d_out), 'dp', across)  31.9 us
    all_to_all x4, starting transfers between devices, bring_back(): lax.all_to_all(rows.reshape(amount * split_ways, CAP, width), 'dp', split...  27.1 us
    all_to_all x4, starting transfers between devices, spread(): lax.all_to_all(sent, 'dp', split_axis=0, concat_axis=0, tiled=True, axis_...  24.7 us
    all_to_all x4, waiting for transfers between devices, reduced(): lax.all_to_all(packed, 'dp', split_axis=0, concat_axis=0, tiled=True, axi...  24.5 us
  transfers between devices with their start and end apart: 21, of which 11 were waited for; matrix products, arithmetic and copies ran while one was open for 32% of the time, Pallas kernels for 0%

profile of v1, /device:TPU:0, one launch (start us, length us, event | category | flops | bytes accessed | tf_op | source)
XLA Modules:
  0.0 628.0 jit_solution(11872852537231392939)
XLA Ops:
  10.9 5.4 all-to-all-start.4
  32.5 31.1 %collective-permute-done.5 = bf16[256,1024]{1,0:T(8,128)(2,1)} collective-permute-done((bf16[256,1024]{1,0:T(8,128)(2,1)}, bf16[256,1024]{1,0:T(8,128)(2,1)}, u32[]{:S(2)}, u32[]{:S(2)}) %collective-permute-start.5) | collective-permute-done | bytes 524320 | tf_op jit(solution)/shard_map/ppermute | solution.py:247
  67.0 7.7 %all-to-all-start.6 = ((bf16[16,80,1024]{2,1,0:T(8,128)(2,1)}), bf16[16,80,1024]{2,1,0:T(8,128)(2,1)}, u32[]{:S(2)}, u32[]{:S(2)}) async-start(bf16[16,80,1024]{2,1,0:T(8,128)(2,1)} %bitcast.205), calls=%async_computation.6 | async-start | bytes 5242880 | tf_op jit(solution)/shard_map/all_to_all | solution.py:91
  96.3 14.8 %all-to-all-done.6 = bf16[16,80,1024]{2,1,0:T(8,128)(2,1)} async-done(((bf16[16,80,1024]{2,1,0:T(8,128)(2,1)}), bf16[16,80,1024]{2,1,0:T(8,128)(2,1)}, u32[]{:S(2)}, u32[]{:S(2)}) %all-to-all-start.6) | async-done | bytes 2621472 | tf_op jit(solution)/shard_map/all_to_all | solution.py:91
  111.1 6.9 %all-to-all-start = ((bf16[16,80,1152]{2,1,0:T(8,128)(2,1)}), bf16[16,80,1152]{2,1,0:T(8,128)(2,1)}, u32[]{:S(2)}, u32[]{:S(2)}) async-start(bf16[16,80,1152]{2,1,0:T(8,128)(2,1)} %bitcast.199), calls=%async_computation | async-start | bytes 5898240 | tf_op jit(solution)/shard_map/all_to_all | solution.py:91
  118.1 54.4 %collective-permute-done.3 = bf16[256,1152]{1,0:T(8,128)(2,1)S(1)} collective-permute-done((bf16[256,1152]{1,0:T(8,128)(2,1)}, bf16[256,1152]{1,0:T(8,128)(2,1)S(1)}, u32[]{:S(2)}, u32[]{:S(2)}) %collective-permute-start.3) | collective-permute-done | bytes 589856 | tf_op jit(solution)/shard_map/ppermute | solution.py:284
  187.0 5.9 copy.260
  197.6 5.9 copy.263
  213.5 8.5 %all-to-all-done.1 = bf16[16,80,1152]{2,1,0:T(8,128)(2,1)} async-done(((bf16[16,80,1152]{2,1,0:T(8,128)(2,1)}), bf16[16,80,1152]{2,1,0:T(8,128)(2,1)}, u32[]{:S(2)}, u32[]{:S(2)}) %all-to-all-start.1) | async-done | bytes 2949152 | tf_op jit(solution)/shard_map/all_to_all | solution.py:91
  255.4 5.4 copy.265
  260.8 6.8 %all-to-all-start.7 = ((bf16[16,80,1152]{2,1,0:T(8,128)(2,1)}), bf16[16,80,1152]{2,1,0:T(8,128)(2,1)}, u32[]{:S(2)}, u32[]{:S(2)}) async-start(bf16[16,80,1152]{2,1,0:T(8,128)(2,1)} %bitcast.201), calls=%async_computation.7 | async-start | bytes 5898240 | tf_op jit(solution)/shard_map/all_to_all | solution.py:98
  267.6 5.4 copy.262
  273.0 36.6 %all-to-all-done.7 = bf16[16,80,1152]{2,1,0:T(8,128)(2,1)} async-done(((bf16[16,80,1152]{2,1,0:T(8,128)(2,1)}), bf16[16,80,1152]{2,1,0:T(8,128)(2,1)}, u32[]{:S(2)}, u32[]{:S(2)}) %all-to-all-start.7) | async-done | bytes 2949152 | tf_op jit(solution)/shard_map/all_to_all | solution.py:98
  309.6 6.6 %all-to-all-start.5 = ((bf16[16,80,1152]{2,1,0:T(8,128)(2,1)}), bf16[16,80,1152]{2,1,0:T(8,128)(2,1)}, u32[]{:S(2)}, u32[]{:S(2)}) async-start(bf16[16,80,1152]{2,1,0:T(8,128)(2,1)} %bitcast.200), calls=%async_computation.5 | async-start | bytes 5898240 | tf_op jit(solution)/shard_map/all_to_all | solution.py:98
  327.9 40.0 %all-to-all-done.5 = bf16[16,80,1152]{2,1,0:T(8,128)(2,1)} async-done(((bf16[16,80,1152]{2,1,0:T(8,128)(2,1)}), bf16[16,80,1152]{2,1,0:T(8,128)(2,1)}, u32[]{:S(2)}, u32[]{:S(2)}) %all-to-all-start.5) | async-done | bytes 2949152 | tf_op jit(solution)/shard_map/all_to_all | solution.py:98
  398.6 6.5 %all_to_all.70 = bf16[2,4,4,32,1152]{4,3,2,1,0:T(8,128)(2,1)} all-to-all(bf16[2,4,4,32,1152]{4,3,2,1,0:T(8,128)(2,1)S(1)} %copy.289), channel_id=1, replica_groups={{0,1},{2,3},{4,5},{6,7},{8,9},{10,11},{12,13},{14,15},{16,17},{18,19},{..., dimensions={0} | all-to-all | bytes 4718592 | tf_op jit(solution)/shard_map/all_to_all | solution.py:155
  405.2 7.5 %all-to-all-start.2 = ((bf16[16,80,1024]{2,1,0:T(8,128)(2,1)}), bf16[16,80,1024]{2,1,0:T(8,128)(2,1)}, u32[]{:S(2)}, u32[]{:S(2)}) async-start(bf16[16,80,1024]{2,1,0:T(8,128)(2,1)} %bitcast.203), calls=%async_computation.2 | async-start | bytes 5242880 | tf_op jit(solution)/shard_map/all_to_all | solution.py:98
  453.9 6.2 all-to-all-start.3
  489.0 6.6 %copy.270 = bf16[1024,2048]{1,0:T(8,128)(2,1)} copy(bf16[1024,2048]{0,1:T(8,128)(2,1)} %pad_maximum_fusion) | data formatting | bytes 8388608 | tf_op jit(solution)/shard_map/concatenate | solution.py:371
  495.6 7.8 %concatenate.93 = bf16[4,4,2,32,2176]{4,3,2,1,0:T(8,128)(2,1)} concatenate(bf16[4,4,2,32,2048]{4,3,2,1,0:T(8,128)(2,1)} %bitcast.197, bf16[4,4,2,32,1]{4,3,2,1,0:T(8,128)(2,1)S(1)} %copy.273, bf16[4,4,2,32,1]{4,3,2,1,0:T(8,128)(2,1)S(1)} %copy-done.39, bf16[4,4,2,32,126]{4,3,2,1,0:T(8,128)(2,1)S(1)} %reshape.328), dimensions={4} | concatenate | bytes 8912896 | tf_op jit(solution)/shard_map/concatenate | solution.py:152
  508.3 30.0 %all_to_all.71 = bf16[2,4,4,32,2176]{4,3,2,1,0:T(8,128)(2,1)} all-to-all(bf16[2,4,4,32,2176]{4,3,2,1,0:T(8,128)(2,1)} %copy.275), channel_id=1, replica_groups={{0,1},{2,3},{4,5},{6,7},{8,9},{10,11},{12,13},{14,15},{16,17},{18,19},{..., dimensions={0} | all-to-all | bytes 8912896 | tf_op jit(solution)/shard_map/all_to_all | solution.py:155
  546.2 7.8 %collective-permute-start.4 = (bf16[256,1024]{1,0:T(8,128)(2,1)}, bf16[256,1024]{1,0:T(8,128)(2,1)}, u32[]{:S(2)}, u32[]{:S(2)}) collective-permute-start(bf16[256,1024]{1,0:T(8,128)(2,1)} %fusion.52), channel_id=1, source_target_pairs={{0,16},{1,17},{2,18},{3,19},{4,20},{5,21},{6,22},{7,23},{8,24},{9,... | collective-permute-start | bytes 1572872 | tf_op jit(solution)/shard_map/ppermute | solution.py:313
  584.7 11.8 %all-to-all-done.9 = bf16[4,4,32,2176]{3,2,1,0:T(8,128)(2,1)} async-done(((bf16[4,4,32,2176]{3,2,1,0:T(8,128)(2,1)}), bf16[4,4,32,2176]{3,2,1,0:T(8,128)(2,1)}, u32[]{:S(2)}, u32[]{:S(2)}) %all-to-all-start.9) | async-done | bytes 2228256 | tf_op jit(solution)/shard_map/all_to_all | solution.py:155
  616.3 9.3 %all-to-all-done.10 = bf16[4,32,2176]{2,1,0:T(8,128)(2,1)S(1)} async-done(((bf16[4,32,2176]{2,1,0:T(8,128)(2,1)}), bf16[4,32,2176]{2,1,0:T(8,128)(2,1)S(1)}, u32[]{:S(2)}, u32[]{:S(2)}) %all-to-all-start.10) | async-done | bytes 557088 | tf_op jit(solution)/shard_map/all_to_all | solution.py:155
  (378 shorter events, 290.3 us)
Async XLA Ops:
  0.6 85.7 %copy-start = (bf16[1024,1024]{1,0:T(8,128)(2,1)S(1)}, bf16[1024,1024]{1,0:T(8,128)(2,1)}, u32[]{:S(2)}) copy-start(bf16[1024,1024]{1,0:T(8,128)(2,1)} %param.21) | copy-start | bytes 6291460
  0.7 5.9 collective-permute-start.2
  7.3 56.4 %copy-start.21 = (pred[1280,256]{1,0:T(32,128)(4,1)}, pred[1280,256]{1,0:T(32,128)(4,1)S(1)}, u32[]{:S(2)}) copy-start(pred[1280,256]{1,0:T(32,128)(4,1)S(1)} %get-tuple-element.64) | copy-start | bytes 983044
  10.9 56.1 %all-to-all-start.4 = ((bf16[16,80,1024]{2,1,0:T(8,128)(2,1)}), bf16[16,80,1024]{2,1,0:T(8,128)(2,1)}, u32[]{:S(2)}, u32[]{:S(2)}) async-start(bf16[16,80,1024]{2,1,0:T(8,128)(2,1)} %bitcast.204), calls=%async_computation.4 | async-start | bytes 5242880 | tf_op jit(solution)/shard_map/all_to_all | solution.py:91
  16.3 47.3 %collective-permute-start.5 = (bf16[256,1024]{1,0:T(8,128)(2,1)}, bf16[256,1024]{1,0:T(8,128)(2,1)}, u32[]{:S(2)}, u32[]{:S(2)}) collective-permute-start(bf16[256,1024]{1,0:T(8,128)(2,1)} %param.27), channel_id=1, source_target_pairs={{0,16},{1,17},{2,18},{3,19},{4,20},{5,21},{6,22},{7,23},{8,24},{9,... | collective-permute-start | bytes 1572872 | tf_op jit(solution)/shard_map/ppermute | solution.py:247
  19.6 55.2 %copy-start.49 = (f32[256]{0:T(256)}, f32[256]{0:T(256)S(1)}, u32[]{:S(2)}) copy-start(f32[256]{0:T(256)S(1)} %fusion.102) | copy-start | bytes 3076
  22.2 59.3 %collective-permute-start = (bf16[256,8,64]{0,2,1:T(8,128)(2,1)}, bf16[256,8,64]{0,2,1:T(8,128)(2,1)}, u32[]{:S(2)}, u32[]{:S(2)}) collective-permute-start(bf16[256,8,64]{0,2,1:T(8,128)(2,1)} %bitcast), channel_id=1, source_target_pairs={{0,1},{1,2},{2,3},{3,4},{4,5},{5,6},{6,7},{7,8},{8,9},{9,10},{10,1... | collective-permute-start | bytes 786440 | tf_op jit(solution)/shard_map/ppermute | solution.py:21
  27.1 50.8 %collective-permute-start.1 = (bf16[256,8,64]{0,2,1:T(8,128)(2,1)S(1)}, bf16[256,8,64]{0,2,1:T(8,128)(2,1)}, u32[]{:S(2)}, u32[]{:S(2)}) collective-permute-start(bf16[256,8,64]{0,2,1:T(8,128)(2,1)S(1)} %fusion.84), channel_id=1, source_target_pairs={{0,1},{1,2},{2,3},{3,4},{4,5},{5,6},{6,7},{7,8},{8,9},{9,10},{10,1... | collective-permute-start | bytes 786440 | tf_op jit(solution)/shard_map/ppermute | solution.py:21
  67.0 44.1 %all-to-all-start.6 = ((bf16[16,80,1024]{2,1,0:T(8,128)(2,1)}), bf16[16,80,1024]{2,1,0:T(8,128)(2,1)}, u32[]{:S(2)}, u32[]{:S(2)}) async-start(bf16[16,80,1024]{2,1,0:T(8,128)(2,1)} %bitcast.205), calls=%async_computation.6 | async-start | bytes 5242880 | tf_op jit(solution)/shard_map/all_to_all | solution.py:91
  111.1 65.0 %all-to-all-start = ((bf16[16,80,1152]{2,1,0:T(8,128)(2,1)}), bf16[16,80,1152]{2,1,0:T(8,128)(2,1)}, u32[]{:S(2)}, u32[]{:S(2)}) async-start(bf16[16,80,1152]{2,1,0:T(8,128)(2,1)} %bitcast.199), calls=%async_computation | async-start | bytes 5898240 | tf_op jit(solution)/shard_map/all_to_all | solution.py:91
  118.0 54.5 %collective-permute-start.3 = (bf16[256,1152]{1,0:T(8,128)(2,1)}, bf16[256,1152]{1,0:T(8,128)(2,1)S(1)}, u32[]{:S(2)}, u32[]{:S(2)}) collective-permute-start(bf16[256,1152]{1,0:T(8,128)(2,1)} %concatenate.86), channel_id=1, source_target_pairs={{0,16},{1,17},{2,18},{3,19},{4,20},{5,21},{6,22},{7,23},{8,24},{9,... | collective-permute-start | bytes 1769480 | tf_op jit(solution)/shard_map/ppermute | solution.py:284
  176.1 45.9 %all-to-all-start.1 = ((bf16[16,80,1152]{2,1,0:T(8,128)(2,1)}), bf16[16,80,1152]{2,1,0:T(8,128)(2,1)}, u32[]{:S(2)}, u32[]{:S(2)}) async-start(bf16[16,80,1152]{2,1,0:T(8,128)(2,1)} %bitcast.198), calls=%async_computation.1 | async-start | bytes 5898240 | tf_op jit(solution)/shard_map/all_to_all | solution.py:91
  260.8 48.8 %all-to-all-start.7 = ((bf16[16,80,1152]{2,1,0:T(8,128)(2,1)}), bf16[16,80,1152]{2,1,0:T(8,128)(2,1)}, u32[]{:S(2)}, u32[]{:S(2)}) async-start(bf16[16,80,1152]{2,1,0:T(8,128)(2,1)} %bitcast.201), calls=%async_computation.7 | async-start | bytes 5898240 | tf_op jit(solution)/shard_map/all_to_all | solution.py:98
  309.6 58.3 %all-to-all-start.5 = ((bf16[16,80,1152]{2,1,0:T(8,128)(2,1)}), bf16[16,80,1152]{2,1,0:T(8,128)(2,1)}, u32[]{:S(2)}, u32[]{:S(2)}) async-start(bf16[16,80,1152]{2,1,0:T(8,128)(2,1)} %bitcast.200), calls=%async_computation.5 | async-start | bytes 5898240 | tf_op jit(solution)/shard_map/all_to_all | solution.py:98
  320.1 50.7 %collective-permute-start.6 = (bf16[256,1152]{1,0:T(8,128)(2,1)}, bf16[256,1152]{1,0:T(8,128)(2,1)}, u32[]{:S(2)}, u32[]{:S(2)}) collective-permute-start(bf16[256,1152]{1,0:T(8,128)(2,1)} %fusion.11), channel_id=1, source_target_pairs={{0,16},{1,17},{2,18},{3,19},{4,20},{5,21},{6,22},{7,23},{8,24},{9,... | collective-permute-start | bytes 1769480 | tf_op jit(solution)/shard_map/ppermute | solution.py:308
  405.2 48.7 %all-to-all-start.2 = ((bf16[16,80,1024]{2,1,0:T(8,128)(2,1)}), bf16[16,80,1024]{2,1,0:T(8,128)(2,1)}, u32[]{:S(2)}, u32[]{:S(2)}) async-start(bf16[16,80,1024]{2,1,0:T(8,128)(2,1)} %bitcast.203), calls=%async_computation.2 | async-start | bytes 5242880 | tf_op jit(solution)/shard_map/all_to_all | solution.py:98
  441.6 38.1 %collective-permute-start.8 = (bf16[256,8,64]{0,2,1:T(8,128)(2,1)}, bf16[256,8,64]{0,2,1:T(8,128)(2,1)}, u32[]{:S(2)}, u32[]{:S(2)}) collective-permute-start(bf16[256,8,64]{0,2,1:T(8,128)(2,1)} %slice.312), channel_id=1, source_target_pairs={{1,0},{2,1},{3,2},{4,3},{5,4},{6,5},{7,6},{8,7},{9,8},{10,9},{11,1... | collective-permute-start | bytes 786440 | tf_op jit(solution)/shard_map/ppermute | solution.py:21
  453.9 54.4 %all-to-all-start.3 = ((bf16[16,80,1024]{2,1,0:T(8,128)(2,1)}), bf16[16,80,1024]{2,1,0:T(8,128)(2,1)}, u32[]{:S(2)}, u32[]{:S(2)}) async-start(bf16[16,80,1024]{2,1,0:T(8,128)(2,1)} %bitcast.202), calls=%async_computation.3 | async-start | bytes 5242880 | tf_op jit(solution)/shard_map/all_to_all | solution.py:98
  471.3 8.2 %collective-permute-start.7 = (bf16[256,8,64]{0,2,1:T(8,128)(2,1)S(1)}, bf16[256,8,64]{0,2,1:T(8,128)(2,1)S(1)}, u32[]{:S(2)}, u32[]{:S(2)}) collective-permute-start(bf16[256,8,64]{0,2,1:T(8,128)(2,1)S(1)} %slice.313), channel_id=1, source_target_pairs={{1,0},{2,1},{3,2},{4,3},{5,4},{6,5},{7,6},{8,7},{9,8},{10,9},{11,1... | collective-permute-start | bytes 786440 | tf_op jit(solution)/shard_map/ppermute | solution.py:21
  538.3 27.0 %all-to-all-start.12 = ((bf16[4,4,32,1152]{3,2,1,0:T(8,128)(2,1)}), bf16[4,4,32,1152]{3,2,1,0:T(8,128)(2,1)}, u32[]{:S(2)}, u32[]{:S(2)}) async-start(bf16[4,4,32,1152]{3,2,1,0:T(8,128)(2,1)} %copy.290), calls=%async_computation.12 | async-start | bytes 2359296 | tf_op jit(solution)/shard_map/all_to_all | solution.py:155
  546.2 32.3 %collective-permute-start.4 = (bf16[256,1024]{1,0:T(8,128)(2,1)}, bf16[256,1024]{1,0:T(8,128)(2,1)}, u32[]{:S(2)}, u32[]{:S(2)}) collective-permute-start(bf16[256,1024]{1,0:T(8,128)(2,1)} %fusion.52), channel_id=1, source_target_pairs={{0,16},{1,17},{2,18},{3,19},{4,20},{5,21},{6,22},{7,23},{8,24},{9,... | collective-permute-start | bytes 1572872 | tf_op jit(solution)/shard_map/ppermute | solution.py:313
  565.3 31.1 %all-to-all-start.9 = ((bf16[4,4,32,2176]{3,2,1,0:T(8,128)(2,1)}), bf16[4,4,32,2176]{3,2,1,0:T(8,128)(2,1)}, u32[]{:S(2)}, u32[]{:S(2)}) async-start(bf16[4,4,32,2176]{3,2,1,0:T(8,128)(2,1)} %copy.280), calls=%async_computation.9 | async-start | bytes 4456448 | tf_op jit(solution)/shard_map/all_to_all | solution.py:155
  596.4 12.1 %all-to-all-start.13 = ((bf16[4,32,1152]{2,1,0:T(8,128)(2,1)}), bf16[4,32,1152]{2,1,0:T(8,128)(2,1)S(1)}, u32[]{:S(2)}, u32[]{:S(2)}) async-start(bf16[4,32,1152]{2,1,0:T(8,128)(2,1)} %concatenate.101), calls=%async_computation.13 | async-start | bytes 589824 | tf_op jit(solution)/shard_map/all_to_all | solution.py:155
  608.6 17.0 %all-to-all-start.10 = ((bf16[4,32,2176]{2,1,0:T(8,128)(2,1)}), bf16[4,32,2176]{2,1,0:T(8,128)(2,1)S(1)}, u32[]{:S(2)}, u32[]{:S(2)}) async-start(bf16[4,32,2176]{2,1,0:T(8,128)(2,1)} %concatenate.95), calls=%async_computation.10 | async-start | bytes 1114112 | tf_op jit(solution)/shard_map/all_to_all | solution.py:155
  (90 other events, 600.9 us)

commit v2 on v1

--- a/solution.py
+++ b/solution.py
@@ -3,6 +3,8 @@
 import jax
 import jax.numpy as jnp
 from jax import lax
+from jax.experimental import pallas as pl
+from jax.experimental.pallas import tpu as pltpu
 from jax.sharding import PartitionSpec as P
 
 HEADS = 16
@@ -111,59 +113,101 @@
     return back, chosen
 
 
-def expert_block(rows, gate, cot_rows, w_gate, w_up, w_down):
-    gate_pre = jnp.dot(rows, w_gate, preferred_element_type=jnp.float32)
-    up_pre = jnp.dot(rows, w_up, preferred_element_type=jnp.float32)
-    sigmoid = jax.nn.sigmoid(gate_pre)
+def expert_kernel(
+    rows_ref, cot_ref, sel_ref, gate_w_ref, up_w_ref, down_w_ref,
+    back_ref, out_ref, hidden_ref, cot_out_ref, grad_gate_ref, grad_up_ref,
+):
+    width = cot_ref.shape[1]
+    rows = rows_ref[:, :width]
+    tail = rows_ref[:, width:].astype(jnp.float32)
+    first, second = sel_ref[0:1, :], sel_ref[1:2, :]
+    gate = jnp.sum(tail * (first + second), axis=1, keepdims=True)
+    gate_pre = jnp.dot(rows, gate_w_ref[...], preferred_element_type=jnp.float32)
+    up_pre = jnp.dot(rows, up_w_ref[...], preferred_element_type=jnp.float32)
+    sigmoid = 1.0 / (1.0 + jnp.exp(-gate_pre))
     activated = gate_pre * sigmoid
     hidden = (activated * up_pre).astype(jnp.bfloat16)
-    cot_float = cot_rows.astype(jnp.float32)
+    hidden_ref[...] = hidden
+    cot_float = cot_ref[...].astype(jnp.float32)
     grad_rows = (gate * cot_float).astype(jnp.bfloat16)
-    grad_hidden = dot_right_t(grad_rows, w_down)
+    cot_out_ref[...] = grad_rows
+    grad_hidden = dot_right_t(grad_rows, down_w_ref[...])
     grad_gate_pre = (grad_hidden * up_pre * (sigmoid * (1.0 + gate_pre * (1.0 - sigmoid)))).astype(
         jnp.bfloat16
     )
     grad_up_pre = (grad_hidden * activated).astype(jnp.bfloat16)
-    back = (dot_right_t(grad_gate_pre, w_gate) + dot_right_t(grad_up_pre, w_up)).astype(
-        jnp.bfloat16
-    )
-    expert_out = jnp.dot(hidden, w_down, preferred_element_type=jnp.float32)
+    grad_gate_ref[...] = grad_gate_pre
+    grad_up_ref[...] = grad_up_pre
+    back = dot_right_t(grad_gate_pre, gate_w_ref[...]) + dot_right_t(grad_up_pre, up_w_ref[...])
+    expert_out = jnp.dot(hidden, down_w_ref[...], preferred_element_type=jnp.float32)
     grad_gates = jnp.sum(expert_out * cot_float, axis=1, keepdims=True)
-    gated_out = (gate * expert_out).astype(jnp.bfloat16)
-    return (hidden, grad_rows, grad_gate_pre, grad_up_pre, back, grad_gates, gated_out)
-
-
-def reduced(parts, extras, devices):
-    sizes = (2, 4, devices // 8)
-    rows = parts.shape[0] // devices
-    width = parts.shape[1]
-    extra_width = extras.shape[1]
-    filler = jnp.zeros((parts.shape[0], 128 - 2 * extra_width), jnp.bfloat16)
-    grid = (sizes[2], sizes[1], sizes[0], rows, -1)
-    main, extra = parts.reshape(grid), extras.reshape(grid)
-    filler = filler.reshape(grid)
+    out_ref[...] = (gate * expert_out).astype(jnp.bfloat16)
+    high = grad_gates.astype(jnp.bfloat16).astype(jnp.float32)
+    back_ref[:, :width] = back.astype(jnp.bfloat16)
+    back_ref[:, width:] = (high * first + (grad_gates - high) * second).astype(jnp.bfloat16)
+
+
+def expert_block(rows, cot_rows, select, w_gate, w_up, w_down):
+    count, wide = rows.shape
+    width, inner = w_gate.shape
+    tile = 4 * CAP
+    by_row = lambda w: pl.BlockSpec((tile, w), lambda i: (i, 0))
+    whole = lambda x: pl.BlockSpec(x.shape, lambda i: (0, 0))
+    shape = lambda w: jax.ShapeDtypeStruct((count, w), jnp.bfloat16)
+    widths = (wide, width, inner, width, inner, inner)
+    return pl.pallas_call(
+        expert_kernel,
+        grid=(count // tile,),
+        in_specs=[
+            by_row(wide), by_row(width), whole(select), whole(w_gate), whole(w_up), whole(w_down)
+        ],
+        out_specs=[by_row(w) for w in widths],
+        out_shape=[shape(w) for w in widths],
+        compiler_params=pltpu.CompilerParams(vmem_limit_bytes=40 * 1024 * 1024),
+        cost_estimate=pl.CostEstimate(
+            flops=14 * count * width * inner,
+            bytes_accessed=2 * (count * (wide + width + sum(widths)) + 3 * width * inner),
+            transcendentals=count * inner,
+        ),
+    )(rows, cot_rows, select, w_gate, w_up, w_down)
+
+
+def halves(values, devices):
+    count, width = values.shape
+    core = lax.axis_index("dp") % 2
+    cut = values.reshape(count, devices // 8, 4, 2, width // devices)
+    cut = cut.transpose(3, 0, 2, 1, 4).reshape(2, count, width // 2)
+    keep = lax.dynamic_index_in_dim(cut, core, 0, keepdims=False)
+    give = lax.dynamic_index_in_dim(cut, 1 - core, 0, keepdims=False)
+    return keep, give
+
+
+def with_partner(keep, give, devices):
+    other = lax.ppermute(give, "dp", [(i, i ^ 1) for i in range(devices)])
+    return jnp.concatenate([keep, other], axis=0)
+
+
+def reduced(left_both, right, devices):
+    right_both = with_partner(right, right, devices)
+    total = dot_left_t(left_both, right_both)
+    width = total.shape[1]
+    rows = 2 * total.shape[0] // devices
     stage_groups = (
-        [[2 * i, 2 * i + 1] for i in range(devices // 2)],
         [[8 * z + 2 * i + c for i in range(4)] for z in range(devices // 8) for c in range(2)],
         [[8 * z + i for z in range(devices // 8)] for i in range(8)],
     )
-    for groups, size in zip(stage_groups, sizes):
-        high, rest = split_two(extra)
-        packed = jnp.concatenate([main.astype(jnp.bfloat16), high, rest, filler], axis=-1)
-        axis = packed.ndim - 3
-        packed = jnp.moveaxis(packed, axis, 0)
+    total = total.reshape(4, devices // 8, rows, width)
+    for groups in stage_groups:
         got = lax.all_to_all(
-            packed, "dp", split_axis=0, concat_axis=0, tiled=True, axis_index_groups=groups
+            total.astype(jnp.bfloat16),
+            "dp",
+            split_axis=0,
+            concat_axis=0,
+            tiled=True,
+            axis_index_groups=groups,
         )
         total = jnp.sum(got.astype(jnp.float32), axis=0)
-        main = total[..., :width]
-        extra = (
-            total[..., width : width + extra_width]
-            + total[..., width + extra_width : width + 2 * extra_width]
-        )
-        filler = filler.reshape((-1,) + filler.shape[-2:])[: math.prod(total.shape[:-2])]
-        filler = filler.reshape(total.shape[:-1] + (filler.shape[-1],))
-    return main, extra
+    return total
 
 
 def block_scores(queries, key_rows, allow, score_scale):
@@ -251,9 +295,9 @@
         member_mask(far_routes, num_experts), half * half_experts, half_experts
     )
     near_cot_rows = spread(near_place, d_out, half_experts, split_ways, half_groups)
-    far_cot_rows = spread(far_place, far_cot, half_experts, split_ways, half_groups)
     x_float = hidden_in.astype(jnp.float32)
     h_one = rms_scale(x_float, attn_gain).astype(jnp.bfloat16)
+    h_one_both = with_partner(*halves(h_one, devices), devices)
     q_raw = jnp.dot(h_one, w_query, preferred_element_type=jnp.float32).reshape(
         tok_count, HEADS, HEAD_DIM
     )
@@ -273,6 +317,8 @@
     q_blocks = q_rot.reshape(tok_count, KV_HEADS, groups, HEAD_DIM)
 
     attended, log_total = forward_block(q_blocks, key_rows, value_rows, allowed, score_scale)
+    attended, far_cot = lax.optimization_barrier((attended, far_cot))
+    far_cot_rows = spread(far_place, far_cot, half_experts, split_ways, half_groups)
     o_low = attended.reshape(tok_count, HEADS * HEAD_DIM).astype(jnp.bfloat16)
     r_one = x_float + jnp.dot(o_low, w_out, preferred_element_type=jnp.float32)
     h_two = rms_scale(r_one, moe_gain).astype(jnp.bfloat16)
@@ -288,34 +334,30 @@
     lane_high = (lane == my_expert)[None, :]
     lane_rest = (lane == my_expert + num_experts)[None, :]
 
-    def work(rows, cot_rows):
-        tail = rows[:, model_width:].astype(jnp.float32)
-        gate = jnp.sum(jnp.where(lane_high | lane_rest, tail, 0.0), axis=1, keepdims=True)
-        rows = rows[:, :model_width]
-        results = expert_block(rows, gate, cot_rows, w_gate, w_up, w_down)
-        high, rest = split_two(results[5])
-        extra = jnp.where(lane_high, high, jnp.where(lane_rest, rest, jnp.bfloat16(0)))
-        return (rows,) + results[:4] + (jnp.concatenate([results[4], extra], axis=1), results[6])
-
-    near = work(near_rows, near_cot_rows)
-    far = work(far_rows, far_cot_rows)
+    select = jnp.concatenate(
+        [lane_high, lane_rest, jnp.zeros((6, 128), jnp.bool_)], axis=0
+    ).astype(jnp.float32)
+    near = expert_block(near_rows, near_cot_rows, select, w_gate, w_up, w_down)
+    near_sent, far_rows = lax.optimization_barrier((near[0], far_rows))
+    far = expert_block(far_rows, far_cot_rows, select, w_gate, w_up, w_down)
 
     def combine(back, chosen):
         return dot_left_t(chosen, back)
 
-    far_back, far_wide = bring_back(far_place, far[5], half_experts, split_ways, half_groups)
-    near_back, near_wide = bring_back(near_place, near[5], half_experts, split_ways, half_groups)
+    near_back, near_wide = bring_back(near_place, near_sent, half_experts, split_ways, half_groups)
+    far_back, far_wide = bring_back(far_place, far[0], half_experts, split_ways, half_groups)
     far_sum = lax.ppermute(combine(far_back, far_wide).astype(jnp.bfloat16), "dp", across)
     grad_tokens = combine(near_back, near_wide) + far_sum.astype(jnp.float32)
-    near_out, far_out, _ = lax.optimization_barrier((near[6], far[6], near_back))
+    near_out, far_out, _ = lax.optimization_barrier((near[1], far[1], far_back))
     far_ret, _ = bring_back(far_place, far_out, half_experts, split_ways, half_groups)
     near_ret, _ = bring_back(near_place, near_out, half_experts, split_ways, half_groups)
     far_mix = lax.ppermute(combine(far_ret, far_wide).astype(jnp.bfloat16), "dp", across)
     mixed = combine(near_ret, near_wide) + far_mix.astype(jnp.float32)
     out_hidden = (r_one + mixed).astype(jnp.bfloat16)
-    grad_down = dot_left_t(near[1], near[2]) + dot_left_t(far[1], far[2])
-    grad_gate = dot_left_t(near[0], near[3]) + dot_left_t(far[0], far[3])
-    grad_up = dot_left_t(near[0], near[4]) + dot_left_t(far[0], far[4])
+    grad_down = dot_left_t(near[2], near[3]) + dot_left_t(far[2], far[3])
+    near_lone, far_lone = near_rows[:, :model_width], far_rows[:, :model_width]
+    grad_gate = dot_left_t(near_lone, near[4]) + dot_left_t(far_lone, far[4])
+    grad_up = dot_left_t(near_lone, near[5]) + dot_left_t(far_lone, far[5])
     cot_float = d_out.astype(jnp.float32)
     grad_h_two = grad_tokens[:, :model_width]
     grad_gates = (
@@ -330,10 +372,8 @@
     grad_r_norm, grad_moe_gain = norm_back_two(grad_h_two)
     grad_r_one = cot_float + grad_r_norm
     grad_y_low = grad_r_one.astype(jnp.bfloat16)
-    grad_out_t = dot_left_t(grad_y_low, o_low)
-    out_part, out_extra = reduced(
-        grad_out_t, jnp.concatenate([grad_router, grad_moe_gain[:, None]], axis=1), devices
-    )
+    grad_y_both = with_partner(*halves(grad_y_low, devices), devices)
+    out_part = reduced(grad_y_both, o_low, devices)
     grad_o_low = dot_right_t(grad_y_low, w_out).astype(jnp.bfloat16)
     grad_o_blocks = grad_o_low.reshape(tok_count, KV_HEADS, groups, HEAD_DIM)
     grad_q_blocks, grad_key_rows, grad_value_rows = backward_block(
@@ -357,9 +397,8 @@
         .astype(jnp.bfloat16)
     )
     grad_v_low = grad_v_rows.reshape(tok_count, KV_HEADS * HEAD_DIM).astype(jnp.bfloat16)
-    grad_query = dot_left_t(h_one, grad_q_low)
-    grad_key = dot_left_t(h_one, grad_k_low)
-    grad_value = dot_left_t(h_one, grad_v_low)
+    shared = jnp.concatenate([grad_q_low, grad_k_low, grad_v_low], axis=1)
+    shared_part = reduced(h_one_both, shared, devices)
     grad_h_one = (
         dot_right_t(grad_q_low, w_query)
         + dot_right_t(grad_k_low, w_key)
@@ -368,16 +407,19 @@
     _, norm_back_one = jax.vjp(rms_scale, x_float, attn_gain)
     grad_x_norm, grad_attn_gain = norm_back_one(grad_h_one)
     grad_input = grad_r_one + grad_x_norm
-    shared = jnp.concatenate([grad_query, grad_key, grad_value], axis=1)
-    shared_part, shared_extra = reduced(shared, grad_attn_gain[:, None], devices)
-    query_width, key_width = grad_query.shape[1], grad_key.shape[1]
+    few = jnp.concatenate(
+        [grad_router, grad_moe_gain[:, None], grad_attn_gain[:, None]], axis=1
+    ).reshape(devices, -1)
+    few = lax.all_to_all(few, "dp", split_axis=0, concat_axis=0, tiled=True)
+    few = jnp.sum(few, axis=0).reshape(-1, num_experts + 2)
+    query_width, key_width = w_query.shape[1], w_key.shape[1]
     grad_query = shared_part[:, :query_width]
     grad_key = shared_part[:, query_width : query_width + key_width]
     grad_value = shared_part[:, query_width + key_width :]
-    grad_attn_gain = shared_extra[:, 0]
+    grad_attn_gain = few[:, num_experts + 1]
     grad_out = out_part.T
-    grad_router = out_extra[:, :num_experts]
-    grad_moe_gain = out_extra[:, num_experts]
+    grad_router = few[:, :num_experts]
+    grad_moe_gain = few[:, num_experts]
     return (
         out_hidden,
         grad_input,

time: 636 us -> 568 us (0.89)
  local copies, waits for them, and re-layouts: 102 us -> 32.2 us
  waiting for transfers between devices: 214 us -> 273 us
  blocking collectives: 36.6 us -> 0 us
  matrix products: 131 us -> 94.9 us
  Pallas kernels: 0 us -> 24.5 us
  other arithmetic: 46.8 us -> 24.6 us
  starting transfers between devices: 95.1 us -> 107 us
    all_to_all x4, waiting for transfers between devices: 23.4 us -> 76.7 us  [spread(): lax.all_to_all(sent, 'dp', split_axis=0, concat_axis=0, tiled=True, axis_...]
    concatenate x10 -> x2, local copies, waits for them, and re-layouts: 41.7 us -> 0.29 us  [the longest x1 0.21 us: local(): jnp.concatenate([grad_router, grad_moe_gain[:, None], grad_attn_gain[:, N...]
    ppermute x1, waiting for transfers between devices: 2.86 us -> 42 us  [local(): lax.ppermute(combine(far_back, far_wide).astype(jnp.bfloat16), 'dp', across)]
    all_to_all x2 -> x0, blocking collectives: 36.6 us -> none  [reduced(): lax.all_to_all(packed, 'dp', split_axis=0, concat_axis=0, tiled=True, axi...]
    ppermute x2, waiting for transfers between devices: 31.9 us -> 4.66 us  [local(): far_routes, far_cot = lax.ppermute((routes, d_out), 'dp', across)]
    pallas_call x0 -> x2, Pallas kernels: none -> 24.5 us  [expert_block(): pl.pallas_call(expert_kernel, grid=(count // tile,), in_specs=[by_row(wid...]
    dot_general x6 -> x0, matrix products: 23.8 us -> none  [the longest x2 8.89 us: expert_block(): up_pre = jnp.dot(rows, w_up, preferred_element_type=jnp.float32)]
    dot_general x11 -> x5, matrix products: 21.2 us -> 5.47 us  [dot_right_t(): lax.dot_general(left, right, (((1,), (1,)), ((), ())), preferred_element_...]
  transfers between devices with their start and end apart: 21 -> 26, of which waited for: 11 -> 14; matrix products, arithmetic and copies ran while one was open for 32% -> 23% of each run, Pallas kernels for 0% -> 4%
where the time goes in v2:
time: 568 us; the launch traced here: 558 us
  waiting for transfers between devices  273 us (48%)
  starting transfers between devices  107 us (19%)
  matrix products  94.9 us (17%)
  local copies, waits for them, and re-layouts  32.2 us (6%)
  other arithmetic  24.6 us (4%)
  Pallas kernels  24.5 us (4%)
    all_to_all x4, waiting for transfers between devices, bring_back(): lax.all_to_all(rows.reshape(amount * split_ways, CAP, width), 'dp', split...  76.7 us
    all_to_all x4, waiting for transfers between devices, spread(): lax.all_to_all(sent, 'dp', split_axis=0, concat_axis=0, tiled=True, axis_...  76.7 us
    dot_general x15, matrix products, dot_left_t(): lax.dot_general(left, right, (((0,), (0,)), ((), ())), preferred_element_...  49.9 us
    ppermute x1, waiting for transfers between devices, local(): far_tokens = lax.ppermute(near_tokens, 'dp', across)  48.8 us
    ppermute x1, waiting for transfers between devices, local(): lax.ppermute(combine(far_back, far_wide).astype(jnp.bfloat16), 'dp', across)  42 us
    all_to_all x4, starting transfers between devices, spread(): lax.all_to_all(sent, 'dp', split_axis=0, concat_axis=0, tiled=True, axis_...  28.7 us
    all_to_all x4, starting transfers between devices, bring_back(): lax.all_to_all(rows.reshape(amount * split_ways, CAP, width), 'dp', split...  27.4 us
    pallas_call x2, Pallas kernels, expert_block(): pl.pallas_call(expert_kernel, grid=(count // tile,), in_specs=[by_row(wid...  24.5 us
  transfers between devices with their start and end apart: 26, of which 14 were waited for; matrix products, arithmetic and copies ran while one was open for 23% of the time, Pallas kernels for 4%

profile of v2, /device:TPU:0, one launch (start us, length us, event | category | flops | bytes accessed | tf_op | source)
XLA Modules:
  0.0 557.5 jit_solution(5328359906345491938)
XLA Ops:
  52.7 21.4 %all-to-all-done.1 = bf16[16,80,1024]{2,1,0:T(8,128)(2,1)} async-done(((bf16[16,80,1024]{2,1,0:T(8,128)(2,1)}), bf16[16,80,1024]{2,1,0:T(8,128)(2,1)}, u32[]{:S(2)}, u32[]{:S(2)}) %all-to-all-start.1) | async-done | bytes 2621472 | tf_op jit(solution)/shard_map/all_to_all | solution.py:93
  74.1 8.0 %all-to-all-start = ((bf16[16,80,1152]{2,1,0:T(8,128)(2,1)}), bf16[16,80,1152]{2,1,0:T(8,128)(2,1)}, u32[]{:S(2)}, u32[]{:S(2)}) async-start(bf16[16,80,1152]{2,1,0:T(8,128)(2,1)} %bitcast.178), calls=%async_computation | async-start | bytes 5898240 | tf_op jit(solution)/shard_map/all_to_all | solution.py:93
  82.1 5.7 %collective-permute-start.4 = (bf16[256,1152]{1,0:T(8,128)(2,1)}, bf16[256,1152]{1,0:T(8,128)(2,1)S(1)}, u32[]{:S(2)}, u32[]{:S(2)}) collective-permute-start(bf16[256,1152]{1,0:T(8,128)(2,1)} %concatenate.71), channel_id=1, source_target_pairs={{0,16},{1,17},{2,18},{3,19},{4,20},{5,21},{6,22},{7,23},{8,24},{9,... | collective-permute-start | bytes 1769480 | tf_op jit(solution)/shard_map/ppermute | solution.py:330
  87.8 48.8 %collective-permute-done.4 = bf16[256,1152]{1,0:T(8,128)(2,1)S(1)} collective-permute-done((bf16[256,1152]{1,0:T(8,128)(2,1)}, bf16[256,1152]{1,0:T(8,128)(2,1)S(1)}, u32[]{:S(2)}, u32[]{:S(2)}) %collective-permute-start.4) | collective-permute-done | bytes 589856 | tf_op jit(solution)/shard_map/ppermute | solution.py:330
  139.3 9.4 %all-to-all-start.2 = ((bf16[16,80,1152]{2,1,0:T(8,128)(2,1)}), bf16[16,80,1152]{2,1,0:T(8,128)(2,1)}, u32[]{:S(2)}, u32[]{:S(2)}) async-start(bf16[16,80,1152]{2,1,0:T(8,128)(2,1)} %bitcast.179), calls=%async_computation.2 | async-start | bytes 5898240 | tf_op jit(solution)/shard_map/all_to_all | solution.py:93
  152.1 38.6 %all-to-all-done.2 = bf16[16,80,1152]{2,1,0:T(8,128)(2,1)} async-done(((bf16[16,80,1152]{2,1,0:T(8,128)(2,1)}), bf16[16,80,1152]{2,1,0:T(8,128)(2,1)}, u32[]{:S(2)}, u32[]{:S(2)}) %all-to-all-start.2) | async-done | bytes 2949152 | tf_op jit(solution)/shard_map/all_to_all | solution.py:93
  190.7 6.8 %all-to-all-start.3 = ((bf16[16,80,1024]{2,1,0:T(8,128)(2,1)}), bf16[16,80,1024]{2,1,0:T(8,128)(2,1)}, u32[]{:S(2)}, u32[]{:S(2)}) async-start(bf16[16,80,1024]{2,1,0:T(8,128)(2,1)} %bitcast.181), calls=%async_computation.3 | async-start | bytes 5242880 | tf_op jit(solution)/shard_map/all_to_all | solution.py:93
  200.1 12.3 %shard_map.229 = (bf16[1280,1152]{1,0:T(8,128)(2,1)}, bf16[1280,1024]{1,0:T(8,128)(2,1)}, bf16[1280,512]{1,0:T(8,128)(2,1)S(1)}, bf16[1280,1024]{1,0:T(8,128)(2,...) custom-call(bf16[1280,1152]{1,0:T(8,128)(2,1)} %bitcast.16.rows_ref, ...), custom_call_target="tpu_custom_call" | custom-call | flops 9395240960 | bytes 20840448 | tf_op jit(solution)/shard_map/pallas_call | solution.py:158
  217.1 16.7 %all-to-all-done.3 = bf16[16,80,1024]{2,1,0:T(8,128)(2,1)} async-done(((bf16[16,80,1024]{2,1,0:T(8,128)(2,1)}), bf16[16,80,1024]{2,1,0:T(8,128)(2,1)}, u32[]{:S(2)}, u32[]{:S(2)}) %all-to-all-start.3) | async-done | bytes 2621472 | tf_op jit(solution)/shard_map/all_to_all | solution.py:93
  233.8 6.8 %all-to-all-start.6 = ((bf16[16,80,1152]{2,1,0:T(8,128)(2,1)}), bf16[16,80,1152]{2,1,0:T(8,128)(2,1)}, u32[]{:S(2)}, u32[]{:S(2)}) async-start(bf16[16,80,1152]{2,1,0:T(8,128)(2,1)} %bitcast.188), calls=%async_computation.6 | async-start | bytes 5898240 | tf_op jit(solution)/shard_map/all_to_all | solution.py:100
  243.1 12.2 %shard_map.230 = (bf16[1280,1152]{1,0:T(8,128)(2,1)}, bf16[1280,1024]{1,0:T(8,128)(2,1)S(1)}, bf16[1280,512]{1,0:T(8,128)(2,1)S(1)}, bf16[1280,1024]{1,0:T(8,128...) custom-call(bf16[1280,1152]{1,0:T(8,128)(2,1)} %bitcast.22.rows_ref, ...), custom_call_target="tpu_custom_call" | custom-call | flops 9395240960 | bytes 20840448 | tf_op jit(solution)/shard_map/pallas_call | solution.py:158
  261.5 21.2 %all-to-all-done.6 = bf16[16,80,1152]{2,1,0:T(8,128)(2,1)} async-done(((bf16[16,80,1152]{2,1,0:T(8,128)(2,1)}), bf16[16,80,1152]{2,1,0:T(8,128)(2,1)}, u32[]{:S(2)}, u32[]{:S(2)}) %all-to-all-start.6) | async-done | bytes 2949152 | tf_op jit(solution)/shard_map/all_to_all | solution.py:100
  282.7 6.6 %all-to-all-start.7 = ((bf16[16,80,1152]{2,1,0:T(8,128)(2,1)}), bf16[16,80,1152]{2,1,0:T(8,128)(2,1)}, u32[]{:S(2)}, u32[]{:S(2)}) async-start(bf16[16,80,1152]{2,1,0:T(8,128)(2,1)} %bitcast.189), calls=%async_computation.7 | async-start | bytes 5898240 | tf_op jit(solution)/shard_map/all_to_all | solution.py:100
  289.3 42.0 %all-to-all-done.7 = bf16[16,80,1152]{2,1,0:T(8,128)(2,1)} async-done(((bf16[16,80,1152]{2,1,0:T(8,128)(2,1)}), bf16[16,80,1152]{2,1,0:T(8,128)(2,1)}, u32[]{:S(2)}, u32[]{:S(2)}) %all-to-all-start.7) | async-done | bytes 2949152 | tf_op jit(solution)/shard_map/all_to_all | solution.py:100
  331.3 7.2 %all-to-all-start.5 = ((bf16[16,80,1024]{2,1,0:T(8,128)(2,1)}), bf16[16,80,1024]{2,1,0:T(8,128)(2,1)}, u32[]{:S(2)}, u32[]{:S(2)}) async-start(bf16[16,80,1024]{2,1,0:T(8,128)(2,1)} %bitcast.177), calls=%async_computation.5 | async-start | bytes 5242880 | tf_op jit(solution)/shard_map/all_to_all | solution.py:100
  345.3 42.0 %collective-permute-done.6 = bf16[256,1152]{1,0:T(8,128)(2,1)} collective-permute-done((bf16[256,1152]{1,0:T(8,128)(2,1)}, bf16[256,1152]{1,0:T(8,128)(2,1)}, u32[]{:S(2)}, u32[]{:S(2)}) %collective-permute-start.6) | collective-permute-done | bytes 589856 | tf_op jit(solution)/shard_map/ppermute | solution.py:349
  397.7 4.8 fusion.44
  403.9 6.7 %all-to-all-start.4 = ((bf16[16,80,1024]{2,1,0:T(8,128)(2,1)}), bf16[16,80,1024]{2,1,0:T(8,128)(2,1)}, u32[]{:S(2)}, u32[]{:S(2)}) async-start(bf16[16,80,1024]{2,1,0:T(8,128)(2,1)} %bitcast.25), calls=%async_computation.4 | async-start | bytes 5242880 | tf_op jit(solution)/shard_map/all_to_all | solution.py:100
  410.6 5.5 fusion
  434.8 13.5 %all-to-all-done.4 = bf16[16,80,1024]{2,1,0:T(8,128)(2,1)} async-done(((bf16[16,80,1024]{2,1,0:T(8,128)(2,1)}), bf16[16,80,1024]{2,1,0:T(8,128)(2,1)}, u32[]{:S(2)}, u32[]{:S(2)}) %all-to-all-start.4) | async-done | bytes 2621472 | tf_op jit(solution)/shard_map/all_to_all | solution.py:100
  448.3 14.3 %all-to-all-start.8 = ((f32[32,1,1088]{2,1,0:T(1,128)}), f32[32,1,1088]{2,1,0:T(1,128)S(1)}, u32[]{:S(2)}, u32[]{:S(2)}) async-start(f32[32,1,1088]{2,1,0:T(1,128)} %all_to_all.56), calls=%async_computation.8 | async-start | bytes 294912 | tf_op jit(solution)/shard_map/all_to_all | solution.py:413
  522.7 4.9 convolution_add_fusion
  530.6 6.9 %all-to-all-done.12 = bf16[4,32,1024]{2,1,0:T(8,128)(2,1)S(1)} async-done(((bf16[4,32,1024]{2,1,0:T(8,128)(2,1)}), bf16[4,32,1024]{2,1,0:T(8,128)(2,1)S(1)}, u32[]{:S(2)}, u32[]{:S(2)}) %all-to-all-start.12) | async-done | bytes 262176 | tf_op jit(solution)/shard_map/all_to_all | solution.py:201
  547.8 8.1 %all-to-all-done.10 = bf16[4,32,2048]{2,1,0:T(8,128)(2,1)S(1)} async-done(((bf16[4,32,2048]{2,1,0:T(8,128)(2,1)}), bf16[4,32,2048]{2,1,0:T(8,128)(2,1)S(1)}, u32[]{:S(2)}, u32[]{:S(2)}) %all-to-all-start.10) | async-done | bytes 524320 | tf_op jit(solution)/shard_map/all_to_all | solution.py:201
  (298 shorter events, 185.0 us)
Async XLA Ops:
  0.7 20.7 %collective-permute-start.3 = (s32[256,8]{0,1:T(8,128)}, s32[256,8]{0,1:T(8,128)S(1)}, u32[]{:S(2)}, u32[]{:S(2)}) collective-permute-start(s32[256,8]{0,1:T(8,128)} %param.16), channel_id=1, source_target_pairs={{0,16},{1,17},{2,18},{3,19},{4,20},{5,21},{6,22},{7,23},{8,24},{9,... | collective-permute-start | bytes 24584 | tf_op jit(solution)/shard_map/ppermute | solution.py:291
  11.1 26.3 %collective-permute-start = (bf16[256,8,64]{0,2,1:T(8,128)(2,1)}, bf16[256,8,64]{0,2,1:T(8,128)(2,1)}, u32[]{:S(2)}, u32[]{:S(2)}) collective-permute-start(bf16[256,8,64]{0,2,1:T(8,128)(2,1)} %bitcast), channel_id=1, source_target_pairs={{0,1},{1,2},{2,3},{3,4},{4,5},{5,6},{6,7},{7,8},{8,9},{9,10},{10,1... | collective-permute-start | bytes 786440 | tf_op jit(solution)/shard_map/ppermute | solution.py:23
  19.5 25.8 %collective-permute-start.2 = (bf16[256,1024]{1,0:T(8,128)(2,1)}, bf16[256,1024]{1,0:T(8,128)(2,1)}, u32[]{:S(2)}, u32[]{:S(2)}) collective-permute-start(bf16[256,1024]{1,0:T(8,128)(2,1)} %param.27), channel_id=1, source_target_pairs={{0,16},{1,17},{2,18},{3,19},{4,20},{5,21},{6,22},{7,23},{8,24},{9,... | collective-permute-start | bytes 1572872 | tf_op jit(solution)/shard_map/ppermute | solution.py:291
  26.1 48.0 %all-to-all-start.1 = ((bf16[16,80,1024]{2,1,0:T(8,128)(2,1)}), bf16[16,80,1024]{2,1,0:T(8,128)(2,1)}, u32[]{:S(2)}, u32[]{:S(2)}) async-start(bf16[16,80,1024]{2,1,0:T(8,128)(2,1)} %bitcast.180), calls=%async_computation.1 | async-start | bytes 5242880 | tf_op jit(solution)/shard_map/all_to_all | solution.py:93
  74.1 65.1 %all-to-all-start = ((bf16[16,80,1152]{2,1,0:T(8,128)(2,1)}), bf16[16,80,1152]{2,1,0:T(8,128)(2,1)}, u32[]{:S(2)}, u32[]{:S(2)}) async-start(bf16[16,80,1152]{2,1,0:T(8,128)(2,1)} %bitcast.178), calls=%async_computation | async-start | bytes 5898240 | tf_op jit(solution)/shard_map/all_to_all | solution.py:93
  82.1 54.5 %collective-permute-start.4 = (bf16[256,1152]{1,0:T(8,128)(2,1)}, bf16[256,1152]{1,0:T(8,128)(2,1)S(1)}, u32[]{:S(2)}, u32[]{:S(2)}) collective-permute-start(bf16[256,1152]{1,0:T(8,128)(2,1)} %concatenate.71), channel_id=1, source_target_pairs={{0,16},{1,17},{2,18},{3,19},{4,20},{5,21},{6,22},{7,23},{8,24},{9,... | collective-permute-start | bytes 1769480 | tf_op jit(solution)/shard_map/ppermute | solution.py:330
  139.3 51.4 %all-to-all-start.2 = ((bf16[16,80,1152]{2,1,0:T(8,128)(2,1)}), bf16[16,80,1152]{2,1,0:T(8,128)(2,1)}, u32[]{:S(2)}, u32[]{:S(2)}) async-start(bf16[16,80,1152]{2,1,0:T(8,128)(2,1)} %bitcast.179), calls=%async_computation.2 | async-start | bytes 5898240 | tf_op jit(solution)/shard_map/all_to_all | solution.py:93
  190.7 43.1 %all-to-all-start.3 = ((bf16[16,80,1024]{2,1,0:T(8,128)(2,1)}), bf16[16,80,1024]{2,1,0:T(8,128)(2,1)}, u32[]{:S(2)}, u32[]{:S(2)}) async-start(bf16[16,80,1024]{2,1,0:T(8,128)(2,1)} %bitcast.181), calls=%async_computation.3 | async-start | bytes 5242880 | tf_op jit(solution)/shard_map/all_to_all | solution.py:93
  233.8 48.8 %all-to-all-start.6 = ((bf16[16,80,1152]{2,1,0:T(8,128)(2,1)}), bf16[16,80,1152]{2,1,0:T(8,128)(2,1)}, u32[]{:S(2)}, u32[]{:S(2)}) async-start(bf16[16,80,1152]{2,1,0:T(8,128)(2,1)} %bitcast.188), calls=%async_computation.6 | async-start | bytes 5898240 | tf_op jit(solution)/shard_map/all_to_all | solution.py:100
  282.7 48.6 %all-to-all-start.7 = ((bf16[16,80,1152]{2,1,0:T(8,128)(2,1)}), bf16[16,80,1152]{2,1,0:T(8,128)(2,1)}, u32[]{:S(2)}, u32[]{:S(2)}) async-start(bf16[16,80,1152]{2,1,0:T(8,128)(2,1)} %bitcast.189), calls=%async_computation.7 | async-start | bytes 5898240 | tf_op jit(solution)/shard_map/all_to_all | solution.py:100
  331.3 72.6 %all-to-all-start.5 = ((bf16[16,80,1024]{2,1,0:T(8,128)(2,1)}), bf16[16,80,1024]{2,1,0:T(8,128)(2,1)}, u32[]{:S(2)}, u32[]{:S(2)}) async-start(bf16[16,80,1024]{2,1,0:T(8,128)(2,1)} %bitcast.177), calls=%async_computation.5 | async-start | bytes 5242880 | tf_op jit(solution)/shard_map/all_to_all | solution.py:100
  342.4 44.9 %collective-permute-start.6 = (bf16[256,1152]{1,0:T(8,128)(2,1)}, bf16[256,1152]{1,0:T(8,128)(2,1)}, u32[]{:S(2)}, u32[]{:S(2)}) collective-permute-start(bf16[256,1152]{1,0:T(8,128)(2,1)} %fusion.9), channel_id=1, source_target_pairs={{0,16},{1,17},{2,18},{3,19},{4,20},{5,21},{6,22},{7,23},{8,24},{9,... | collective-permute-start | bytes 1769480 | tf_op jit(solution)/shard_map/ppermute | solution.py:349
  344.8 120.1 %collective-permute-start.12 = (bf16[256,1024]{0,1:T(8,128)(2,1)}, bf16[256,1024]{0,1:T(8,128)(2,1)}, u32[]{:S(2)}, u32[]{:S(2)}) collective-permute-start(bf16[256,1024]{0,1:T(8,128)(2,1)} %bitcast.205), channel_id=1, source_target_pairs={{0,1},{1,0},{2,3},{3,2},{4,5},{5,4},{6,7},{7,6},{8,9},{9,8},{10,11... | collective-permute-start | bytes 1572872 | tf_op jit(solution)/shard_map/ppermute | solution.py:186
  397.7 67.2 %collective-permute-start.11 = (bf16[256,512]{0,1:T(8,128)(2,1)S(1)}, bf16[256,512]{0,1:T(8,128)(2,1)}, u32[]{:S(2)}, u32[]{:S(2)}) collective-permute-start(bf16[256,512]{0,1:T(8,128)(2,1)S(1)} %get-tuple-element.61), channel_id=1, source_target_pairs={{0,1},{1,0},{2,3},{3,2},{4,5},{5,4},{6,7},{7,6},{8,9},{9,8},{10,11... | collective-permute-start | bytes 786440 | tf_op jit(solution)/shard_map/ppermute | solution.py:186
  402.6 26.0 %collective-permute-start.8 = (bf16[256,8,64]{0,2,1:T(8,128)(2,1)S(1)}, bf16[256,8,64]{0,2,1:T(8,128)(2,1)}, u32[]{:S(2)}, u32[]{:S(2)}) collective-permute-start(bf16[256,8,64]{0,2,1:T(8,128)(2,1)S(1)} %slice.161), channel_id=1, source_target_pairs={{1,0},{2,1},{3,2},{4,3},{5,4},{6,5},{7,6},{8,7},{9,8},{10,9},{11,1... | collective-permute-start | bytes 786440 | tf_op jit(solution)/shard_map/ppermute | solution.py:23
  403.9 44.4 %all-to-all-start.4 = ((bf16[16,80,1024]{2,1,0:T(8,128)(2,1)}), bf16[16,80,1024]{2,1,0:T(8,128)(2,1)}, u32[]{:S(2)}, u32[]{:S(2)}) async-start(bf16[16,80,1024]{2,1,0:T(8,128)(2,1)} %bitcast.25), calls=%async_computation.4 | async-start | bytes 5242880 | tf_op jit(solution)/shard_map/all_to_all | solution.py:100
  448.3 22.7 %all-to-all-start.8 = ((f32[32,1,1088]{2,1,0:T(1,128)}), f32[32,1,1088]{2,1,0:T(1,128)S(1)}, u32[]{:S(2)}, u32[]{:S(2)}) async-start(f32[32,1,1088]{2,1,0:T(1,128)} %all_to_all.56), calls=%async_computation.8 | async-start | bytes 294912 | tf_op jit(solution)/shard_map/all_to_all | solution.py:413
  463.6 21.1 %collective-permute-start.10 = (bf16[256,2048]{0,1:T(8,128)(2,1)}, bf16[256,2048]{0,1:T(8,128)(2,1)}, u32[]{:S(2)}, u32[]{:S(2)}) collective-permute-start(bf16[256,2048]{0,1:T(8,128)(2,1)} %pad_maximum_fusion.1), channel_id=1, source_target_pairs={{0,1},{1,0},{2,3},{3,2},{4,5},{5,4},{6,7},{7,6},{8,9},{9,8},{10,11... | collective-permute-start | bytes 3145736 | tf_op jit(solution)/shard_map/ppermute | solution.py:186
  464.7 20.0 %collective-permute-start.9 = (bf16[256,512]{0,1:T(8,128)(2,1)}, bf16[256,512]{0,1:T(8,128)(2,1)S(1)}, u32[]{:S(2)}, u32[]{:S(2)}) collective-permute-start(bf16[256,512]{0,1:T(8,128)(2,1)} %get-tuple-element.63), channel_id=1, source_target_pairs={{0,1},{1,0},{2,3},{3,2},{4,5},{5,4},{6,7},{7,6},{8,9},{9,8},{10,11... | collective-permute-start | bytes 786440 | tf_op jit(solution)/shard_map/ppermute | solution.py:186
  471.0 18.7 %all-to-all-start.11 = ((bf16[4,4,32,1024]{3,2,1,0:T(8,128)(2,1)}), bf16[4,4,32,1024]{3,2,1,0:T(8,128)(2,1)}, u32[]{:S(2)}, u32[]{:S(2)}) async-start(bf16[4,4,32,1024]{3,2,1,0:T(8,128)(2,1)} %bitcast.203), calls=%async_computation.11 | async-start | bytes 2097152 | tf_op jit(solution)/shard_map/all_to_all | solution.py:201
  489.7 29.7 %all-to-all-start.9 = ((bf16[4,4,32,2048]{3,2,1,0:T(8,128)(2,1)}), bf16[4,4,32,2048]{3,2,1,0:T(8,128)(2,1)}, u32[]{:S(2)}, u32[]{:S(2)}) async-start(bf16[4,4,32,2048]{3,2,1,0:T(8,128)(2,1)} %bitcast.198), calls=%async_computation.9 | async-start | bytes 4194304 | tf_op jit(solution)/shard_map/all_to_all | solution.py:201
  507.0 34.0 %collective-permute-start.5 = (bf16[256,1024]{1,0:T(8,128)(2,1)}, bf16[256,1024]{1,0:T(8,128)(2,1)}, u32[]{:S(2)}, u32[]{:S(2)}) collective-permute-start(bf16[256,1024]{1,0:T(8,128)(2,1)} %fusion.49), channel_id=1, source_target_pairs={{0,16},{1,17},{2,18},{3,19},{4,20},{5,21},{6,22},{7,23},{8,24},{9,... | collective-permute-start | bytes 1572872 | tf_op jit(solution)/shard_map/ppermute | solution.py:354
  519.3 18.2 %all-to-all-start.12 = ((bf16[4,32,1024]{2,1,0:T(8,128)(2,1)}), bf16[4,32,1024]{2,1,0:T(8,128)(2,1)S(1)}, u32[]{:S(2)}, u32[]{:S(2)}) async-start(bf16[4,32,1024]{2,1,0:T(8,128)(2,1)} %reduce_sum.178), calls=%async_computation.12 | async-start | bytes 524288 | tf_op jit(solution)/shard_map/all_to_all | solution.py:201
  537.5 18.4 %all-to-all-start.10 = ((bf16[4,32,2048]{2,1,0:T(8,128)(2,1)}), bf16[4,32,2048]{2,1,0:T(8,128)(2,1)S(1)}, u32[]{:S(2)}, u32[]{:S(2)}) async-start(bf16[4,32,2048]{2,1,0:T(8,128)(2,1)} %reduce_sum.176), calls=%async_computation.10 | async-start | bytes 1048576 | tf_op jit(solution)/shard_map/all_to_all | solution.py:201
  (83 other events, 590.7 us)
